TPU v7x, 128 devices: a whole 4x4x4 slice. The times are simulated.
128 devices in a mesh: sp: 4 (over x_hi, core), vel: 32 (over x_lo, y, z).
Axes of the slice: x: 4 (x_hi: 2, x_lo: 2; x = x_hi * 2 + x_lo), y: 4, z: 4, core: 2. Of those that a mesh axis runs over, the one named last changes fastest.
Arguments:
- prior: float32 [4, 4, 4, 4096, 512], P(None, None, None, 'vel', 'sp'), may hold values from -50 to 50
- block_inverse: float32 [4096, 64, 64], P('vel'), may hold values from -0.2 to 0.7
Outputs:
- iterate: float32 [4, 4, 4, 4096, 512], P(None, None, None, 'vel', 'sp')
All inputs are finite; a program needn't handle non-finite values.
Results may differ from a plain program's by a relative error of at most 0.0001.
Values sent between devices are 32-bit elements; how exact they have to be, the bound alone decides.
No kernel may reach another device: no remote copies, remote signals or barrier semaphores. Data moves between devices by JAX's collectives and lax.ppermute only.
A program may use at most 128 MiB of HBM per device.

v0:
```python
import jax
import jax.numpy as jnp
from jax import lax
from jax.sharding import PartitionSpec as P

NV1 = 16
NY = 8
NZ = 8
ITERS = 2


COLLISION = 1.0
COUPLING = 0.25
LID_SPEED = 0.6
HIGHEST = lax.Precision.HIGHEST


def extended(cells, sides, width):
    for axis, dim in sides:
        count = lax.axis_size(axis)
        ends = count - 1
        head = lax.slice_in_dim(cells, 0, width, axis=dim)
        tail = lax.slice_in_dim(cells, cells.shape[dim] - width, cells.shape[dim], axis=dim)
        cells = jnp.concatenate(
            [
                lax.ppermute(tail, axis, [(i, (i + 1) % count) for i in range(ends)]),
                cells,
                lax.ppermute(head, axis, [((i + 1) % count, i) for i in range(ends)]),
            ],
            axis=dim,
        )
    return cells


def velocity_grid(points):
    total = points * points * points
    serial = jnp.arange(total, dtype=jnp.int32)
    spacing = 6.0 / points
    centre = 0.5 * (points - 1)
    speed_x = ((serial // (points * points)).astype(jnp.float32) - centre) * spacing
    speed_y = ((serial // points % points).astype(jnp.float32) - centre) * spacing
    speed_z = ((serial % points).astype(jnp.float32) - centre) * spacing
    return (speed_x, speed_y, speed_z)


def moment_tables(points):
    speed_x, speed_y, speed_z = velocity_grid(points)
    square = speed_x * speed_x + speed_y * speed_y + speed_z * speed_z
    rows = [
        jnp.ones_like(square),
        speed_x,
        speed_y,
        speed_z,
        speed_x * speed_x - 1.0,
        speed_y * speed_y - 1.0,
        speed_z * speed_z - 1.0,
        speed_x * speed_y,
        speed_x * speed_z,
        speed_y * speed_z,
        (square - 5.0) * speed_x,
        (square - 5.0) * speed_y,
        (square - 5.0) * speed_z,
    ]
    polynomials = jnp.stack(rows)
    density = jnp.exp(-0.5 * square)
    density = density / jnp.sum(density)
    weighted = polynomials * density
    scaled = polynomials / jnp.sum(weighted * polynomials, axis=1, keepdims=True)
    return (weighted, scaled, speed_x, speed_y, speed_z)


def face_tables(mode_count):
    degree = jnp.arange(mode_count, dtype=jnp.int32)
    face_high = jnp.sqrt(degree.astype(jnp.float32) + 0.5)
    face_low = jnp.where(degree % 2 == 0, 1.0, -1.0).astype(jnp.float32) * face_high
    return (face_high, face_low)


def face_trace(values, field_part, direction):
    return jnp.tensordot(values, field_part, axes=([0], [direction]), precision=HIGHEST)


def lift_face(values, face_value, direction):
    shape = [1] * (face_value.ndim + 1)
    shape[direction] = values.shape[0]
    return jnp.expand_dims(face_value, direction) * values.reshape(shape)


def wall_face(wall_value, mode_count, cell_count):
    corner = (jnp.arange(mode_count, dtype=jnp.int32) == 0).astype(jnp.float32)
    pattern = 2.0 * corner[:, None] * corner[None, :]
    return (
        pattern[:, :, None, None]
        * wall_value[None, None, :, None]
        * jnp.ones((1, 1, 1, cell_count), jnp.float32)
    )


def from_below(face_value, stride, incoming):
    return jnp.concatenate([incoming, face_value[..., : face_value.shape[-1] - stride]], axis=-1)


def from_above(face_value, stride, incoming):
    return jnp.concatenate([face_value[..., stride:], incoming], axis=-1)


def direction_term(
    lower_raw,
    upper_raw,
    coordinate,
    extent,
    speed,
    lower_wall,
    upper_wall,
    direction,
    face_high,
    face_low,
):
    mode_count = face_high.shape[0]
    cell_count = lower_raw.shape[-1]
    lower_face = jnp.where(coordinate > 0, lower_raw, wall_face(lower_wall, mode_count, cell_count))
    upper_face = jnp.where(
        coordinate < extent - 1, upper_raw, wall_face(upper_wall, mode_count, cell_count)
    )
    forward = jnp.maximum(speed, 0.0)[:, None]
    backward = jnp.maximum(-speed, 0.0)[:, None]
    return lift_face(face_low, forward * lower_face, direction) + lift_face(
        face_high, backward * upper_face, direction
    )


def body(prior, block_inverse):
    mode_count = prior.shape[0]
    vel_dev = prior.shape[3]
    cell_count = prior.shape[4]
    basis = mode_count**3
    plane_size = NY * NZ
    slab_cells = cell_count // plane_size
    face_high, face_low = face_tables(mode_count)
    weighted, scaled, speed_x, speed_y, speed_z = moment_tables(NV1)
    first = lax.axis_index("vel") * vel_dev
    weighted = lax.dynamic_slice_in_dim(weighted, first, vel_dev, 1)
    scaled = lax.dynamic_slice_in_dim(scaled, first, vel_dev, 1)
    speeds = tuple(
        (
            lax.dynamic_slice_in_dim(component, first, vel_dev, 0)
            for component in (speed_x, speed_y, speed_z)
        )
    )
    cell_index = jnp.arange(cell_count, dtype=jnp.int32)
    coords = (
        lax.axis_index("sp") * slab_cells + cell_index // plane_size,
        cell_index // NZ % NY,
        cell_index % NZ,
    )
    extents = (lax.axis_size("sp") * slab_cells, NY, NZ)
    strides = (plane_size, NZ, 1)
    unit_wall = jnp.ones_like(speeds[0])
    lid_wall = jnp.exp(LID_SPEED * speeds[0] - 0.5 * LID_SPEED * LID_SPEED)
    upper_walls = (unit_wall, unit_wall, lid_wall)
    iterate = prior
    for iteration in range(ITERS):
        partial_sum = jnp.einsum(
            "kv,pvc->kpc", weighted, iterate.reshape(basis, vel_dev, cell_count), precision=HIGHEST
        )
        moments = lax.psum(partial_sum, "vel")
        equilibrium = jnp.einsum("kv,kpc->pvc", scaled, moments, precision=HIGHEST).reshape(
            iterate.shape
        )
        right_side = prior + COLLISION * equilibrium
        widened = extended(iterate, (("sp", 4),), plane_size)
        upward = face_trace(face_high, widened, 0)
        downward = face_trace(face_low, widened, 0)
        lower_raw = upward[..., :cell_count]
        upper_raw = downward[..., 2 * plane_size :]
        right_side = right_side + COUPLING * direction_term(
            lower_raw,
            upper_raw,
            coords[0],
            extents[0],
            speeds[0],
            unit_wall,
            upper_walls[0],
            0,
            face_high,
            face_low,
        )
        for direction in (1, 2):
            upward = face_trace(face_high, iterate, direction)
            downward = face_trace(face_low, iterate, direction)
            empty_plane = jnp.zeros(upward.shape[:-1] + (strides[direction],), jnp.float32)
            lower_raw = from_below(upward, strides[direction], empty_plane)
            upper_raw = from_above(downward, strides[direction], empty_plane)
            right_side = right_side + COUPLING * direction_term(
                lower_raw,
                upper_raw,
                coords[direction],
                extents[direction],
                speeds[direction],
                unit_wall,
                upper_walls[direction],
                direction,
                face_high,
                face_low,
            )
        flat = right_side.reshape(basis, vel_dev, cell_count)
        iterate = jnp.einsum("vpq,qvc->pvc", block_inverse, flat, precision=HIGHEST).reshape(
            prior.shape
        )
    return iterate


def solution(mesh):
    return jax.shard_map(
        body,
        mesh=mesh,
        in_specs=(P(None, None, None, "vel", "sp"), P("vel", None, None)),
        out_specs=P(None, None, None, "vel", "sp"),
        check_vma=False,
    )
```

profile of v0, /device:TPU:0, one launch (start us, length us, event | category | flops | bytes accessed | tf_op | source)
XLA Modules:
  0.0 867.2 jit_solution(7938925791161687650)
XLA Ops:
  6.5 8.1 fusion.142
  34.7 12.7 %fusion.26 = f32[1,4,4,128,128]{4,0,3,2,1:T(1,128)S(1)} fusion(f32[4,4,4,128,128]{4,3,2,1,0:T(8,128)} %param.2), kind=kOutput, calls=%fused_computation.30 | convolution fusion | flops 12582956 | bytes 5242880 | tf_op jit(solution)/shard_map/dot_general | solution.py:80
  47.5 8.9 %fusion.22 = f32[1,4,4,128,128]{4,0,3,2,1:T(1,128)S(1)} fusion(f32[4,4,4,128,128]{4,3,2,1,0:T(8,128)S(1)} %copy-done), kind=kOutput, calls=%fused_computation.26 | convolution fusion | flops 12582956 | bytes 5242880 | tf_op jit(solution)/shard_map/dot_general | solution.py:80
  63.8 12.8 %fusion.28 = f32[1,4,4,128,128]{4,0,3,2,1:T(1,128)S(1)} fusion(f32[4,4,4,128,128]{4,3,2,1,0:T(8,128)} %param.2), kind=kOutput, calls=%fused_computation.32 | convolution fusion | flops 12582920 | bytes 5242880 | tf_op jit(solution)/shard_map/dot_general | solution.py:80
  76.5 9.0 %fusion.24 = f32[1,4,4,128,128]{4,0,3,2,1:T(1,128)S(1)} fusion(f32[4,4,4,128,128]{4,3,2,1,0:T(8,128)S(1)} %copy-done.1), kind=kOutput, calls=%fused_computation.28 | convolution fusion | flops 12582920 | bytes 5242880 | tf_op jit(solution)/shard_map/dot_general | solution.py:80
  85.5 261.5 %all-reduce.11.cloned.1.call-done = f32[13,64,128]{2,0,1:T(8,128)} async-done(((f32[13,64,128]{2,0,1:T(8,128)}), f32[13,64,128]{2,0,1:T(8,128)}) %all-reduce.11.cloned.1.call-update) | async-done | bytes 426000 | tf_op jit(solution)/shard_map/psum | solution.py:166
  347.0 9.4 %fusion.70 = f32[64,128,128]{2,1,0:T(8,128)} fusion(f32[13,64,128]{2,0,1:T(8,128)} %all-reduce.11.cloned.1.call-done, f32[13,4096]{1,0:T(8,128)S(1)} %stack.2, s32[]{:T(128)S(6)} %select_n.393, f32[13]{0:T(128)S(1)} %get-tuple-element.9), kind=kOutput, calls=%fused_computation.120 | convolution fusion | flops 163579520 | bytes 4628996 | tf_op jit(solution)/shard_map/kv,kpc->pvc/dot_general | solution.py:167
  369.4 6.8 pad_maximum_fusion
  376.2 19.5 %fusion.4 = f32[1,4,4,128,256]{4,0,3,2,1:T(1,128)S(1)} fusion(f32[4,4,4,128,256]{4,3,2,1,0:T(8,128)S(1)} %pad_maximum_fusion), kind=kOutput, calls=%fused_computation.6 | convolution fusion | flops 25165868 | bytes 10485760 | tf_op jit(solution)/shard_map/dot_general | solution.py:80
  395.7 19.8 %fusion.6 = f32[1,4,4,128,256]{4,0,3,2,1:T(1,128)S(1)} fusion(f32[4,4,4,128,256]{4,3,2,1,0:T(8,128)S(1)} %pad_maximum_fusion), kind=kOutput, calls=%fused_computation.8 | convolution fusion | flops 25165832 | bytes 10485760 | tf_op jit(solution)/shard_map/dot_general | solution.py:80
  423.2 6.9 fusion.12
  430.1 6.2 fusion.141
  450.3 7.2 fusion.8
  457.6 9.5 %fusion.14 = f32[1,4,4,128,128]{4,0,3,2,1:T(1,128)S(1)} fusion(f32[4,4,4,128,128]{4,2,1,0,3:T(4,128)} %bitcast.118), kind=kOutput, calls=%fused_computation.18 | convolution fusion | flops 12582956 | bytes 5242880 | tf_op jit(solution)/shard_map/dot_general | solution.py:80
  467.5 7.9 fusion.18
  475.4 8.1 fusion.20
  485.3 8.1 fusion.16
  493.4 274.7 %all-reduce.13.cloned.1.call-done = f32[13,64,128]{2,0,1:T(8,128)} async-done(((f32[13,64,128]{2,0,1:T(8,128)}), f32[13,64,128]{2,0,1:T(8,128)}) %all-reduce.13.cloned.1.call-update) | async-done | bytes 426000 | tf_op jit(solution)/shard_map/psum | solution.py:166
  768.1 9.5 %fusion.68 = f32[64,128,128]{2,1,0:T(8,128)} fusion(f32[13,64,128]{2,0,1:T(8,128)} %all-reduce.13.cloned.1.call-done, f32[13,4096]{1,0:T(8,128)S(1)} %stack.2, s32[]{:T(128)S(6)} %select_n.393, f32[13]{0:T(128)S(1)} %get-tuple-element.9), kind=kOutput, calls=%fused_computation.119 | convolution fusion | flops 163579520 | bytes 4628996 | tf_op jit(solution)/shard_map/kv,kpc->pvc/dot_general | solution.py:167
  777.5 5.3 copy.17
  792.8 9.7 %pad_maximum_fusion.1 = f32[4,4,4,128,256]{4,2,1,0,3:T(4,128)S(1)} fusion(f32[4,4,4,128,64]{4,2,1,0,3:T(4,128)} %copy.21, f32[4,4,4,128,128]{4,2,1,0,3:T(4,128)} %bitcast.119, f32[4,4,4,128,64]{4,2,1,0,3:T(4,128)} %copy.20), kind=kLoop, calls=%fused_computation.1 | loop fusion | flops 4194304 | bytes 16777216 | tf_op jit(solution)/shard_map/concatenate | solution.py:24
  802.6 19.2 %fusion = f32[1,4,4,128,256]{4,0,3,2,1:T(1,128)S(1)} fusion(f32[4,4,4,128,256]{4,2,1,0,3:T(4,128)S(1)} %pad_maximum_fusion.1), kind=kOutput, calls=%fused_computation.2 | convolution fusion | flops 25165868 | bytes 10485760 | tf_op jit(solution)/shard_map/dot_general | solution.py:80
  821.7 19.0 %fusion.2 = f32[1,4,4,128,256]{4,0,3,2,1:T(1,128)S(1)} fusion(f32[4,4,4,128,256]{4,2,1,0,3:T(4,128)S(1)} %pad_maximum_fusion.1), kind=kOutput, calls=%fused_computation.4 | convolution fusion | flops 25165832 | bytes 10485760 | tf_op jit(solution)/shard_map/dot_general | solution.py:80
  848.2 7.5 fusion.10
  (91 shorter events, 85.6 us)
Async XLA Ops:
  6.5 340.5 %all-reduce.11.cloned.1.call-start = ((), (), s32[]{:S(2)}) async-start(), calls=%async_computation | async-start | bytes 1048576 | tf_op jit(solution)/shard_map/psum | solution.py:166
  18.4 343.2 %collective-permute-start = (f32[4,4,4,128,64]{3,4,2,1,0:T(8,128)}, f32[4,4,4,128,64]{3,4,2,1,0:T(8,128)}, u32[]{:S(2)}, u32[]{:S(2)}) collective-permute-start(f32[4,4,4,128,64]{3,4,2,1,0:T(8,128)} %copy.56), channel_id=1, source_target_pairs={{0,32},{32,64},{64,96},{1,33},{33,65},{65,97},{2,34},{34,66},{66,9... | collective-permute-start | bytes 6291464 | tf_op jit(solution)/shard_map/ppermute | solution.py:26
  24.9 340.7 %collective-permute-start.1 = (f32[4,4,4,128,64]{3,4,2,1,0:T(8,128)}, f32[4,4,4,128,64]{3,4,2,1,0:T(8,128)}, u32[]{:S(2)}, u32[]{:S(2)}) collective-permute-start(f32[4,4,4,128,64]{3,4,2,1,0:T(8,128)} %copy.57), channel_id=1, source_target_pairs={{32,0},{64,32},{96,64},{33,1},{65,33},{97,65},{34,2},{66,34},{98,6... | collective-permute-start | bytes 6291464 | tf_op jit(solution)/shard_map/ppermute | solution.py:28
  28.5 0.7 copy-start.13
  34.3 733.8 %all-reduce.13.cloned.1.call-start = ((), (), s32[]{:S(2)}) async-start(), calls=%async_computation.1 | async-start | bytes 1048576 | tf_op jit(solution)/shard_map/psum | solution.py:166
  34.6 12.8 %copy-start = (f32[4,4,4,128,128]{4,3,2,1,0:T(8,128)S(1)}, f32[4,4,4,128,128]{4,3,2,1,0:T(8,128)}, u32[]{:S(2)}) copy-start(f32[4,4,4,128,128]{4,3,2,1,0:T(8,128)} %param.2) | copy-start | bytes 12582916
  47.5 10.7 %copy-start.12 = (f32[128,64,64]{0,2,1:T(8,128)S(1)}, f32[128,64,64]{0,2,1:T(8,128)}, u32[]{:S(2)}) copy-start(f32[128,64,64]{0,2,1:T(8,128)} %param.3) | copy-start | bytes 6291460
  63.7 12.8 %copy-start.1 = (f32[4,4,4,128,128]{4,3,2,1,0:T(8,128)S(1)}, f32[4,4,4,128,128]{4,3,2,1,0:T(8,128)}, u32[]{:S(2)}) copy-start(f32[4,4,4,128,128]{4,3,2,1,0:T(8,128)} %param.2) | copy-start | bytes 12582916
  415.5 1.2 copy-start.10
  416.7 2.2 copy-start.2
  416.7 3.5 copy-start.9
  420.2 2.9 copy-start.6
  430.1 6.2 copy-start.4
  441.3 341.6 %collective-permute-start.2 = (f32[4,4,4,128,64]{3,4,2,1,0:T(8,128)}, f32[4,4,4,128,64]{3,4,2,1,0:T(8,128)}, u32[]{:S(2)}, u32[]{:S(2)}) collective-permute-start(f32[4,4,4,128,64]{3,4,2,1,0:T(8,128)} %copy.58), channel_id=1, source_target_pairs={{0,32},{32,64},{64,96},{1,33},{33,65},{65,97},{2,34},{34,66},{66,9... | collective-permute-start | bytes 6291464 | tf_op jit(solution)/shard_map/ppermute | solution.py:26
  448.9 339.0 %collective-permute-start.3 = (f32[4,4,4,128,64]{3,4,2,1,0:T(8,128)}, f32[4,4,4,128,64]{3,4,2,1,0:T(8,128)}, u32[]{:S(2)}, u32[]{:S(2)}) collective-permute-start(f32[4,4,4,128,64]{3,4,2,1,0:T(8,128)} %copy.59), channel_id=1, source_target_pairs={{32,0},{64,32},{96,64},{33,1},{65,33},{97,65},{34,2},{66,34},{98,6... | collective-permute-start | bytes 6291464 | tf_op jit(solution)/shard_map/ppermute | solution.py:28
  457.6 9.9 %copy-start.5 = (f32[128,128,64]{1,2,0:T(8,128)S(1)}, f32[128,128,64]{1,2,0:T(8,128)}, u32[]{:S(2)}) copy-start(f32[128,128,64]{1,2,0:T(8,128)} %copy-done.4) | copy-start | bytes 12582916
  840.7 1.2 copy-start.11
  842.0 2.2 copy-start.3
  842.0 3.5 copy-start.8
  845.4 2.8 copy-start.7
Sparse Core Ops, SparseCore 0:
  34.4 312.5 all-reduce.10
  457.7 310.3 all-reduce.12
where the time goes:
time: 873 us; the launch traced here: 867 us
  waiting for transfers between devices  536 us (61%)
  matrix products  200 us (23%)
  local copies, waits for them, and re-layouts  81 us (9%)
  other arithmetic  27.5 us (3%)
  between operations  14.1 us (2%)
    psum x2, waiting for transfers between devices, body(): moments = lax.psum(partial_sum, 'vel')  536 us
    dot_general x12, matrix products, face_trace(): jnp.tensordot(values, field_part, axes=([0], [direction]), precision=HIGH...  155 us
    unnamed x33, local copies, waits for them, and re-layouts  29.6 us
    dot_general x2, matrix products, body(): jnp.einsum('kv,kpc->pvc', scaled, moments, precision=HIGHEST)  18.9 us
  transfers between devices with their start and end apart: 6, of which 2 were waited for; matrix products, arithmetic and copies ran while one was open for 17% of the time, Pallas kernels for 0%

commit v1 on v0

v1 whole, which is shorter than its diff:
```python
import functools

import jax
import jax.numpy as jnp
import numpy as np
from jax import lax
from jax.experimental import pallas as pl
from jax.experimental.pallas import tpu as pltpu
from jax.sharding import PartitionSpec as P

NV1 = 16
ITERS = 2
COUPLING = 0.25
LID_SPEED = 0.6
STEP = 6.0 / NV1
CENTRE = 0.5 * (NV1 - 1)
VEL = 32
LOCAL_Y = 8
HIGH = [float(np.sqrt(k + 0.5)) for k in range(4)]
HIGHEST = lax.Precision.HIGHEST
F32 = jnp.float32
BF16 = jnp.bfloat16
HALF = 64


def grid_speed(index):
    return (np.asarray(index, np.float64) - CENTRE) * STEP


def local_polynomials(y, z):
    r2 = y * y + z * z
    return [np.ones_like(r2), y, z, y * y, z * z, y * z, r2 * y, r2 * z]


def combination(x):
    c = np.zeros((13, 8))
    c[0, 0] = 1.0
    c[1, 0] = x
    c[2, 1] = 1.0
    c[3, 2] = 1.0
    c[4, 0] = x * x - 1.0
    c[5, 3], c[5, 0] = 1.0, -1.0
    c[6, 4], c[6, 0] = 1.0, -1.0
    c[7, 1] = x
    c[8, 2] = x
    c[9, 5] = 1.0
    c[10, 0], c[10, 3], c[10, 4] = x * (x * x - 5.0), x, x
    c[11, 1], c[11, 6] = x * x - 5.0, 1.0
    c[12, 2], c[12, 7] = x * x - 5.0, 1.0
    return c


def tables():
    speed = grid_speed(np.arange(NV1))
    weight = np.exp(-0.5 * speed * speed)
    weight = weight / weight.sum()
    x, y, z = np.meshgrid(speed, speed, speed, indexing="ij")
    w = weight[:, None, None] * weight[None, :, None] * weight[None, None, :]
    g = np.stack(local_polynomials(y, z))
    per_x = np.stack([combination(s) for s in speed])
    h = np.einsum("xkj,jxyz->kxyz", per_x, g)
    norm = (w * h * h).sum(axis=(1, 2, 3))
    source = np.repeat(per_x * weight[:, None, None], 2, axis=0)
    target = np.repeat(per_x, 2, axis=0)
    mix = np.einsum("tkj,k,ski->tjsi", target, 1.0 / norm, source).reshape(VEL * 8, VEL * 8)
    local = np.zeros((2, 8, 128))
    for part in range(2):
        ys = speed[part * LOCAL_Y : (part + 1) * LOCAL_Y]
        yy, zz = np.meshgrid(ys, speed, indexing="ij")
        wy = weight[part * LOCAL_Y : (part + 1) * LOCAL_Y]
        ww = wy[:, None] * weight[None, :]
        local[part] = np.stack([(ww * p).reshape(-1) for p in local_polynomials(yy, zz)])
    scalars = np.zeros((VEL, 24))
    for i in range(VEL):
        vx = speed[i // 2]
        part = i % 2
        scalars[i, 0] = 1.0 if vx > 0 else -1.0
        scalars[i, 1] = 1.0 if part else -1.0
        scalars[i, 2] = COUPLING * abs(vx)
        scalars[i, 3] = 2.0 * np.exp(LID_SPEED * vx - 0.5 * LID_SPEED * LID_SPEED)
        scalars[i, 8:16] = speed[part * LOCAL_Y : (part + 1) * LOCAL_Y]
        scalars[i, 16:24] = weight[part * LOCAL_Y : (part + 1) * LOCAL_Y]
    return mix.astype(np.float32), local.astype(np.float32), scalars.astype(np.float32), speed, weight


MIX, LOCAL, SCALARS, SPEED, WEIGHT = tables()


def split(a):
    hi = a.astype(BF16)
    return hi, (a - hi.astype(F32)).astype(BF16)


def lane_index(shape):
    return lax.broadcasted_iota(jnp.int32, shape, len(shape) - 1)


def outgoing_mask(lane, sign):
    return jnp.where(sign > 0, lane, 2 * HALF - 1 - lane) >= HALF


def trace_face(sign):
    return [HIGH[k] if k % 2 == 0 else HIGH[k] * sign for k in range(4)]


def lift_faces(sign):
    return [HIGH[k] if k % 2 == 0 else -HIGH[k] * sign for k in range(4)]


def first_moments_kernel(place, scalars, local_ref, prior_ref, moments_ref, send_ref):
    step = pl.program_id(0)
    vel = place[0]
    sign = scalars[vel, 0]
    face = trace_face(sign)
    weights = local_ref[vel % 2]
    traces = []
    for half in range(2):
        trace = None
        for p0 in range(4):
            block = prior_ref[p0, half, 0]
            hi, lo = split(block)
            both = jnp.concatenate([hi, lo], axis=0)
            product = jnp.dot(weights, both, preferred_element_type=F32)
            moments_ref[p0, half, 0] = product[:8] + product[8:]
            term = face[p0] * block
            trace = term if trace is None else trace + term
        traces.append(trace)
    mask = outgoing_mask(lane_index(traces[0].shape), sign)
    send_ref[pl.ds(step, 128, stride=8), :] = jnp.where(mask, traces[1], pltpu.roll(traces[0], HALF, 1))


def first_moments(place, scalars, local, prior):
    view = prior.reshape(4, 2, 8, 128, 128)
    moments, send = pl.pallas_call(
        first_moments_kernel,
        grid=(8,),
        in_specs=[
            pl.BlockSpec(memory_space=pltpu.SMEM),
            pl.BlockSpec(memory_space=pltpu.SMEM),
            pl.BlockSpec((2, 16, 256), lambda i: (0, 0, 0)),
            pl.BlockSpec((4, 2, 1, 128, 128), lambda i: (0, 0, i, 0, 0)),
        ],
        out_specs=[
            pl.BlockSpec((4, 2, 1, 8, 128), lambda i: (0, 0, i, 0, 0)),
            pl.BlockSpec((1024, 128), lambda i: (0, 0)),
        ],
        out_shape=[
            jax.ShapeDtypeStruct((4, 2, 8, 8, 128), F32),
            jax.ShapeDtypeStruct((1024, 128), F32),
        ],
        compiler_params=pltpu.CompilerParams(vmem_limit_bytes=48 * 2**20),
        name="first_moments",
    )(place, scalars, local, view)
    return moments.reshape(VEL, 16, 128), send


def mix_kernel(mix_ref, in_ref, out_ref):
    for low in range(2):
        part = in_ref[:, low * 8 : low * 8 + 8, :].reshape(VEL * 8, 128)
        mixed = jnp.dot(mix_ref[...], part, preferred_element_type=F32, precision=HIGHEST)
        out_ref[:, low * 8 : low * 8 + 8, :] = mixed.reshape(VEL, 8, 128)


def mix_moments(mix, partial_sums):
    return pl.pallas_call(
        mix_kernel,
        out_shape=jax.ShapeDtypeStruct((VEL, 16, 128), F32),
        name="mix_moments",
    )(mix, partial_sums)


def sum_over_velocities(mix, partial_sums):
    gathered = lax.all_to_all(partial_sums, "vel", 0, 0)
    mixed = mix_moments(mix, gathered)
    return lax.all_to_all(mixed, "vel", 0, 0)


def inflow_yz(source, base, target, scalars, vel, y):
    lane = lane_index((8, 128))
    sublane = lax.broadcasted_iota(jnp.int32, (8, 128), 0)
    sign_y = scalars[vel, 1]
    trace_y, lift_y = trace_face(sign_y), lift_faces(sign_y)
    up_y = sign_y > 0
    shift_y = jnp.where(up_y, 8, 120)
    cell_y = jnp.where(up_y, lane // 8 % 8, 7 - lane // 8 % 8)
    scale_y = jnp.where(cell_y > 0, COUPLING * jnp.abs(y), 0.0)
    wall_y = jnp.where(cell_y > 0, 0.0, 2.0 * COUPLING * jnp.abs(y))
    for part in range(2):
        rows = pl.ds(part * 8, 8)
        up = part == 1
        speed = jnp.abs((sublane + (part * 8)).astype(F32) - CENTRE) * (STEP * COUPLING)
        inside = (lane % 8 > 0) if up else (lane % 8 < 7)
        scale_z = jnp.where(inside, speed, 0.0)
        wall_z = jnp.where(inside, 0.0, speed * (2.0 if up else scalars[vel, 3]))
        trace_z, lift_z = trace_face(1.0 if up else -1.0), lift_faces(1.0 if up else -1.0)
        for p0 in range(4):
            x = [[source[p0 * 16 + p1 * 4 + p2, rows, :] for p2 in range(4)] for p1 in range(4)]
            face_y, face_z = [], []
            for k in range(4):
                ty = sum(trace_y[p1] * x[p1][k] for p1 in range(4))
                ty = pltpu.roll(ty, shift_y, 1) * scale_y
                tz = sum(trace_z[p2] * x[k][p2] for p2 in range(4))
                tz = pltpu.roll(tz, 1 if up else 127, 1) * scale_z
                if p0 == 0 and k == 0:
                    ty = ty + wall_y
                    tz = tz + wall_z
                face_y.append(ty)
                face_z.append(tz)
            for p1 in range(4):
                for p2 in range(4):
                    q = p0 * 16 + p1 * 4 + p2
                    value = base[q, rows, :] + lift_y[p1] * face_y[p2] + lift_z[p2] * face_z[p1]
                    target[q * 16 + part * 8 : q * 16 + part * 8 + 8, :] = value


def own_inflow_x(column, place, scalars, vel, mask):
    sign = scalars[vel, 0]
    face, lift = trace_face(sign), lift_faces(sign)
    trace = sum(face[p0] * column[p0 * 16 : p0 * 16 + 16] for p0 in range(4))
    turned = pltpu.roll(trace, HALF, 1)
    send = jnp.where(mask[:8], trace[8:], turned[:8])
    row = lax.broadcasted_iota(jnp.int32, (16, 128), 0)
    wall = jnp.where(row == 0, scalars_wall(place, sign), 0.0)
    own = jnp.where(mask, turned, wall) * scalars[vel, 2]
    return send, jnp.concatenate([lift[p0] * own for p0 in range(4)], axis=0)


def scalars_wall(place, sign):
    last = jnp.where(sign > 0, 0, place[2] - 1)
    return jnp.where(place[1] == last, 2.0, 0.0)


def prepare_kernel(place, scalars, prior_ref, inverse_ref, right_ref, packed_ref, scratch):
    step = pl.program_id(0)
    vel = place[0]
    inflow_yz(prior_ref, prior_ref, scratch, scalars, vel, scalars[vel, 8 + step])
    flat = prior_ref.reshape(1024, 128)
    mask = outgoing_mask(lane_index((16, 128)), scalars[vel, 0])
    lane = lane_index((64, 128))
    for v in range(16):
        _, own = own_inflow_x(flat[pl.ds(v, 64, stride=16), :], place, scalars, vel, mask)
        right_ref[v] = scratch[pl.ds(v, 64, stride=16), :] + own
        block = inverse_ref[v]
        hi, lo = split(jnp.concatenate([block, block], axis=1))
        packed_ref[v] = jnp.where(lane < HALF, hi.astype(F32), lo.astype(F32)).astype(BF16)


def prepare(place, scalars, prior, inverse):
    return pl.pallas_call(
        prepare_kernel,
        grid=(8,),
        in_specs=[
            pl.BlockSpec(memory_space=pltpu.SMEM),
            pl.BlockSpec(memory_space=pltpu.SMEM),
            pl.BlockSpec((64, 16, 128), lambda i: (0, i, 0)),
            pl.BlockSpec((16, 64, 64), lambda i: (i, 0, 0)),
        ],
        out_specs=[
            pl.BlockSpec((16, 64, 128), lambda i: (i, 0, 0)),
            pl.BlockSpec((16, 64, 128), lambda i: (i, 0, 0)),
        ],
        out_shape=[
            jax.ShapeDtypeStruct((128, 64, 128), F32),
            jax.ShapeDtypeStruct((128, 64, 128), BF16),
        ],
        scratch_shapes=[pltpu.VMEM((1024, 128), F32)],
        compiler_params=pltpu.CompilerParams(vmem_limit_bytes=48 * 2**20),
        name="prepare",
    )(place, scalars, prior, inverse)


def relax(scalars, vel, step, right_ref, packed_ref, recv_ref, mixed_ref, planes, columns, mask, store):
    @pl.when(step == 0)
    def _():
        for j in range(8):
            planes[j] = mixed_ref[pl.ds(j, 64, stride=8), :]

    y = scalars[vel, 8 + step]
    e = [planes[j] for j in range(8)]
    columns[0] = e[0] + y * (e[1] + y * (e[3] + y * e[6]))
    columns[1] = e[2] + y * (e[5] + y * e[7])
    columns[2] = e[4] + y * e[6]
    columns[3] = e[7]
    sign = scalars[vel, 0]
    lift = lift_faces(sign)
    for v in range(16):
        z = float(SPEED[v])
        equilibrium = columns[0] + z * (columns[1] + z * (columns[2] + z * columns[3]))
        recv = recv_ref[v]
        both = jnp.concatenate([recv, pltpu.roll(recv, HALF, 1)], axis=0)
        edge = jnp.where(mask, 0.0, both) * scalars[vel, 2]
        inflow = jnp.concatenate([lift[p0] * edge for p0 in range(4)], axis=0)
        hi, lo = split(right_ref[v] + equilibrium + inflow)
        packed = packed_ref[v]
        fresh = jnp.dot(
            jnp.concatenate([packed, packed], axis=1),
            jnp.concatenate([hi, hi, lo, lo], axis=0),
            preferred_element_type=F32,
        )
        store(v, fresh)


def middle_kernel(
    place, scalars, prior_ref, right_ref, packed_ref, recv_ref, mixed_ref,
    next_ref, send_ref, moments_ref,
    planes, columns, fresh_rows, scratch, own_rows, sums,
):
    step = pl.program_id(0)
    vel = place[0]
    mask = outgoing_mask(lane_index((16, 128)), scalars[vel, 0])
    totals = []

    def store(v, fresh):
        fresh_rows[pl.ds(v, 64, stride=16), :] = fresh
        send, own = own_inflow_x(fresh, place, scalars, vel, mask)
        send_ref[v] = send
        own_rows[v] = own
        z = float(SPEED[v])
        for k in range(4):
            term = (float(WEIGHT[v]) * z**k) * fresh
            if v == 0:
                sums[k] = term
            else:
                sums[k] = sums[k] + term

    relax(scalars, vel, step, right_ref, packed_ref, recv_ref, mixed_ref, planes, columns, mask, store)
    y = scalars[vel, 8 + step]
    weight = scalars[vel, 16 + step]
    s = [weight * sums[k] for k in range(4)]
    y2 = y * y
    totals = [s[0], y * s[0], s[1], y2 * s[0], s[2], y * s[1], y * (y2 * s[0] + s[2]), s[3] + y2 * s[1]]

    for j in range(8):
        rows = pl.ds(j, 64, stride=8)

        @pl.when(step == 0)
        def _(j=j, rows=rows):
            moments_ref[rows, :] = totals[j]

        @pl.when(step > 0)
        def _(j=j, rows=rows):
            moments_ref[rows, :] = moments_ref[rows, :] + totals[j]

    inflow_yz(fresh_rows.reshape(64, 16, 128), prior_ref, scratch, scalars, vel, y)
    for v in range(16):
        next_ref[v] = scratch[pl.ds(v, 64, stride=16), :] + own_rows[v]


def middle(place, scalars, prior, right, packed, recv, mixed):
    next_right, send, moments = pl.pallas_call(
        middle_kernel,
        grid=(8,),
        in_specs=[
            pl.BlockSpec(memory_space=pltpu.SMEM),
            pl.BlockSpec(memory_space=pltpu.SMEM),
            pl.BlockSpec((64, 16, 128), lambda i: (0, i, 0)),
            pl.BlockSpec((16, 64, 128), lambda i: (i, 0, 0)),
            pl.BlockSpec((16, 64, 128), lambda i: (i, 0, 0)),
            pl.BlockSpec((16, 8, 128), lambda i: (i, 0, 0)),
            pl.BlockSpec((512, 128), lambda i: (0, 0)),
        ],
        out_specs=[
            pl.BlockSpec((16, 64, 128), lambda i: (i, 0, 0)),
            pl.BlockSpec((16, 8, 128), lambda i: (i, 0, 0)),
            pl.BlockSpec((512, 128), lambda i: (0, 0)),
        ],
        out_shape=[
            jax.ShapeDtypeStruct((128, 64, 128), F32),
            jax.ShapeDtypeStruct((128, 8, 128), F32),
            jax.ShapeDtypeStruct((512, 128), F32),
        ],
        scratch_shapes=[
            pltpu.VMEM((8, 64, 128), F32),
            pltpu.VMEM((4, 64, 128), F32),
            pltpu.VMEM((1024, 128), F32),
            pltpu.VMEM((1024, 128), F32),
            pltpu.VMEM((16, 64, 128), F32),
            pltpu.VMEM((4, 64, 128), F32),
        ],
        compiler_params=pltpu.CompilerParams(vmem_limit_bytes=48 * 2**20),
        name="middle",
    )(place, scalars, prior, right, packed, recv, mixed)
    return next_right, send, moments.reshape(VEL, 16, 128)


def last_kernel(place, scalars, right_ref, packed_ref, recv_ref, mixed_ref, out_ref, planes, columns):
    step = pl.program_id(0)
    vel = place[0]
    mask = outgoing_mask(lane_index((16, 128)), scalars[vel, 0])
    flat = out_ref.reshape(1024, 128)

    def store(v, fresh):
        flat[pl.ds(v, 64, stride=16), :] = fresh

    relax(scalars, vel, step, right_ref, packed_ref, recv_ref, mixed_ref, planes, columns, mask, store)


def last(place, scalars, right, packed, recv, mixed):
    return pl.pallas_call(
        last_kernel,
        grid=(8,),
        in_specs=[
            pl.BlockSpec(memory_space=pltpu.SMEM),
            pl.BlockSpec(memory_space=pltpu.SMEM),
            pl.BlockSpec((16, 64, 128), lambda i: (i, 0, 0)),
            pl.BlockSpec((16, 64, 128), lambda i: (i, 0, 0)),
            pl.BlockSpec((16, 8, 128), lambda i: (i, 0, 0)),
            pl.BlockSpec((512, 128), lambda i: (0, 0)),
        ],
        out_specs=pl.BlockSpec((64, 16, 128), lambda i: (0, i, 0)),
        out_shape=jax.ShapeDtypeStruct((64, 128, 128), F32),
        scratch_shapes=[pltpu.VMEM((8, 64, 128), F32), pltpu.VMEM((4, 64, 128), F32)],
        compiler_params=pltpu.CompilerParams(vmem_limit_bytes=48 * 2**20),
        name="last",
    )(place, scalars, right, packed, recv, mixed)


def halo_pairs(slabs):
    pairs = []
    for slab in range(slabs):
        for vel in range(VEL):
            other = slab + 1 if SCALARS[vel, 0] > 0 else slab - 1
            if 0 <= other < slabs:
                pairs.append((slab * VEL + vel, other * VEL + vel))
    return pairs


def body(slabs, prior, block_inverse):
    shape = prior.shape
    cells = prior.reshape(64, 128, 128)
    place = jnp.stack([lax.axis_index("vel"), lax.axis_index("sp"), jnp.int32(slabs)]).astype(jnp.int32)
    scalars = jnp.asarray(SCALARS)
    hi = LOCAL.astype(jnp.bfloat16)
    lo = (LOCAL - hi.astype(np.float32)).astype(jnp.bfloat16)
    local = jnp.asarray(
        np.concatenate([np.concatenate([hi, hi], axis=2), np.concatenate([lo, lo], axis=2)], axis=1)
    )
    mix = jnp.asarray(MIX)
    axes = ("sp", "vel")
    pairs = halo_pairs(slabs)

    moments, send = first_moments(place, scalars, local, cells)
    recv = lax.ppermute(send, axes, pairs).reshape(128, 8, 128)
    mixed = sum_over_velocities(mix, moments).reshape(512, 128)
    right, packed = prepare(place, scalars, cells, block_inverse)
    right, send, moments = middle(place, scalars, cells, right, packed, recv, mixed)
    recv = lax.ppermute(send, axes, pairs)
    mixed = sum_over_velocities(mix, moments).reshape(512, 128)
    return last(place, scalars, right, packed, recv, mixed).reshape(shape)


def solution(mesh):
    spec = P(None, None, None, "vel", "sp")
    return jax.shard_map(
        functools.partial(body, mesh.shape["sp"]),
        mesh=mesh,
        in_specs=(spec, P("vel", None, None)),
        out_specs=spec,
        check_vma=False,
    )
```

time: 873 us -> 105 us (0.12)
  the two profiles are of different devices: /device:TPU:0 before, /device:TPU:1 now
where the time goes in v1:
time: 105 us; the launch traced here: 103 us
  blocking collectives  48.9 us (47%)
  Pallas kernels  37.1 us (35%)
  starting transfers between devices  9.11 us (9%)
  local copies, waits for them, and re-layouts  8.11 us (8%)
    all_to_all x2, blocking collectives, sum_over_velocities(): gathered = lax.all_to_all(partial_sums, 'vel', 0, 0)  37.1 us
    pallas_call x1, Pallas kernels, middle(): pl.pallas_call(middle_kernel, grid=(8,), in_specs=[pl.BlockSpec(memory_sp...  12.3 us
    all_to_all x1, blocking collectives, sum_over_velocities(): return lax.all_to_all(mixed, 'vel', 0, 0)  11.8 us
    pallas_call x1, Pallas kernels, prepare(): pl.pallas_call(prepare_kernel, grid=(8,), in_specs=[pl.BlockSpec(memory_s...  9.17 us
    pallas_call x1, Pallas kernels, last(): pl.pallas_call(last_kernel, grid=(8,), in_specs=[pl.BlockSpec(memory_spac...  8.28 us
    unnamed x11, local copies, waits for them, and re-layouts  8.11 us
    pallas_call x2, Pallas kernels, mix_moments(): pl.pallas_call(mix_kernel, out_shape=jax.ShapeDtypeStruct((VEL, 16, 128),...  4.63 us
    all_to_all x1, starting transfers between devices, sum_over_velocities(): return lax.all_to_all(mixed, 'vel', 0, 0)  3.87 us
  transfers between devices with their start and end apart: 3, of which 0 were waited for; matrix products, arithmetic and copies ran while one was open for 4% of the time, Pallas kernels for 13%

profile of v1, /device:TPU:1, one launch (start us, length us, event | category | flops | bytes accessed | tf_op | source)
XLA Modules:
  0.0 103.3 jit_solution(342773432544403514)
XLA Ops:
  0.0 0.1 pad_add_fusion.place
  0.1 0.0 copy-start
  0.1 2.2 %copy-done = f32[4,4,4,128,128]{4,3,2,1,0:T(8,128)S(1)} copy-done((f32[4,4,4,128,128]{4,3,2,1,0:T(8,128)S(1)}, f32[4,4,4,128,128]{4,3,2,1,0:T(8,128)}, u32[]{:S(2)}) %copy-start) | copy-done | bytes 4194328
  2.3 0.7 copy-done.1
  3.0 0.7 copy-done.3
  3.7 2.7 %first_moments.1 = (f32[4,2,8,8,128]{4,3,2,1,0:T(8,128)S(1)}, f32[1024,128]{1,0:T(8,128)S(1)}) custom-call(s32[3]{0:T(128)S(1)} %pad_add_fusion.place, f32[32,24]{1,0:T(8,128)S(1)} %copy-done.1, bf16[2,16,256]{2,1,0:T(8,128)(2,1)S(1)} %copy-done.3, f32[4,2,8,128,128]{4,3,2,1,0:T(8,128)S(1)} %bitcast.12), custom_call_target="tpu_custom_call" | custom-call | tf_op jit(solution)/shard_map/first_moments/pallas_call | solution.py:134
  6.4 0.0 copy-start.2
  6.4 3.3 %collective-permute-start = (f32[1024,128]{1,0:T(8,128)S(1)}, f32[1024,128]{1,0:T(8,128)S(1)}, u32[]{:S(2)}, u32[]{:S(2)}) collective-permute-start(f32[1024,128]{1,0:T(8,128)S(1)} %get-tuple-element.14), channel_id=1, source_target_pairs={{16,48},{17,49},{18,50},{19,51},{20,52},{21,53},{22,54},{23,55},{2... | collective-permute-start | bytes 1572872 | tf_op jit(solution)/shard_map/ppermute | solution.py:443
  9.8 19.0 %all_to_all.20.in_ref = f32[32,16,128]{2,1,0:T(8,128)} all-to-all(f32[32,16,128]{2,1,0:T(8,128)S(1)} %bitcast.17), channel_id=1, replica_groups=mesh['sp'=4,'vel'=32] {'vel'}, dimensions={0} | all-to-all | bytes 524288 | tf_op jit(solution)/shard_map/all_to_all | solution.py:173
  28.7 2.3 %mix_moments.2 = f32[32,16,128]{2,1,0:T(8,128)} custom-call(f32[256,256]{1,0:T(8,128)} %constant.19.clone.mix_ref, f32[32,16,128]{2,1,0:T(8,128)} %all_to_all.20.in_ref), custom_call_target="tpu_custom_call" | custom-call | tf_op jit(solution)/shard_map/mix_moments/pallas_call | solution.py:165
  31.0 3.9 %all-to-all-start.1 = ((f32[32,16,128]{2,1,0:T(8,128)}), f32[32,16,128]{2,1,0:T(8,128)S(1)}, u32[]{:S(2)}, u32[]{:S(2)}) async-start(f32[32,16,128]{2,1,0:T(8,128)} %mix_moments.2), calls=%async_computation.1 | async-start | bytes 524288 | tf_op jit(solution)/shard_map/all_to_all | solution.py:175
  34.9 0.0 copy-done.4
  34.9 4.5 %copy.6.inverse_ref = f32[128,64,64]{2,1,0:T(8,128)} copy(f32[128,64,64]{0,2,1:T(8,128)S(1)} %copy-done.4) | data formatting | bytes 4194304 | tf_op args[1]
  39.4 0.0 copy-done.2
  39.4 9.2 %prepare.1 = (f32[128,64,128]{2,1,0:T(8,128)}, bf16[128,64,128]{2,1,0:T(8,128)(2,1)S(1)}) custom-call(s32[3]{0:T(128)S(1)} %pad_add_fusion.place, f32[32,24]{1,0:T(8,128)S(1)} %copy-done.2, f32[64,128,128]{2,1,0:T(8,128)} %bitcast.10, f32[128,64,64]{2,1,0:T(8,128)} %copy.6.inverse_ref), custom_call_target="tpu_custom_call" | custom-call | tf_op jit(solution)/shard_map/prepare/pallas_call | solution.py:249
  48.6 0.0 all-to-all-done.1
  48.6 0.0 collective-permute-done
  48.6 12.3 %middle.1 = (f32[128,64,128]{2,1,0:T(8,128)}, f32[128,8,128]{2,1,0:T(8,128)S(1)}, f32[512,128]{1,0:T(8,128)S(1)}) custom-call(s32[3]{0:T(128)S(1)} %pad_add_fusion.place, f32[32,24]{1,0:T(8,128)S(1)} %copy-done.2, f32[64,128,128]{2,1,0:T(8,128)} %bitcast.11, f32[128,64,128]{2,1,0:T(8,128)} %get-tuple-element.12.right_ref, ...), custom_call_target="tpu_custom_call" | custom-call | tf_op jit(solution)/shard_map/middle/pallas_call | solution.py:350
  60.9 1.9 %collective-permute-start.1 = (f32[128,8,128]{2,1,0:T(8,128)S(1)}, f32[128,8,128]{2,1,0:T(8,128)S(1)}, u32[]{:S(2)}, u32[]{:S(2)}) collective-permute-start(f32[128,8,128]{2,1,0:T(8,128)S(1)} %get-tuple-element.17), channel_id=1, source_target_pairs={{16,48},{17,49},{18,50},{19,51},{20,52},{21,53},{22,54},{23,55},{2... | collective-permute-start | bytes 1572872 | tf_op jit(solution)/shard_map/ppermute | solution.py:447
  62.8 18.1 %all_to_all.21.in_ref = f32[32,16,128]{2,1,0:T(8,128)} all-to-all(f32[32,16,128]{2,1,0:T(8,128)S(1)} %bitcast.16), channel_id=1, replica_groups=mesh['sp'=4,'vel'=32] {'vel'}, dimensions={0} | all-to-all | bytes 524288 | tf_op jit(solution)/shard_map/all_to_all | solution.py:173
  80.9 2.3 %mix_moments.3 = f32[32,16,128]{2,1,0:T(8,128)} custom-call(f32[256,256]{1,0:T(8,128)} %constant.19.clone.mix_ref, f32[32,16,128]{2,1,0:T(8,128)} %all_to_all.21.in_ref), custom_call_target="tpu_custom_call" | custom-call | tf_op jit(solution)/shard_map/mix_moments/pallas_call | solution.py:165
  83.2 11.8 %all_to_all.22 = f32[32,16,128]{2,1,0:T(8,128)S(1)} all-to-all(f32[32,16,128]{2,1,0:T(8,128)} %mix_moments.3), channel_id=1, replica_groups=mesh['sp'=4,'vel'=32] {'vel'}, dimensions={0} | all-to-all | bytes 524288 | tf_op jit(solution)/shard_map/all_to_all | solution.py:175
  95.0 0.0 collective-permute-done.1.recv_ref
  95.1 8.3 %last.1 = f32[64,128,128]{2,1,0:T(8,128)} custom-call(s32[3]{0:T(128)S(1)} %pad_add_fusion.place, f32[32,24]{1,0:T(8,128)S(1)} %copy-done.2, f32[128,64,128]{2,1,0:T(8,128)} %get-tuple-element.16.right_ref, bf16[128,64,128]{2,1,0:T(8,128)(2,1)S(1)} %get-tuple-element.13.packed_ref, f32[128,8,128]{2,1,0:T(8,128)S(1)} %collective-permute-done.1.recv_ref, ...), custom_call_target="tpu_custom_call" | custom-call | tf_op jit(solution)/shard_map/last/pallas_call | solution.py:399
  (3 shorter events, 0.0 us)
Async XLA Ops:
  0.1 2.2 %copy-start = (f32[4,4,4,128,128]{4,3,2,1,0:T(8,128)S(1)}, f32[4,4,4,128,128]{4,3,2,1,0:T(8,128)}, u32[]{:S(2)}) copy-start(f32[4,4,4,128,128]{4,3,2,1,0:T(8,128)} %param.5) | copy-start | bytes 12582916
  2.3 0.7 copy-start.1
  3.0 0.7 copy-start.3
  3.7 31.2 %copy-start.4 = (f32[128,64,64]{0,2,1:T(8,128)S(1)}, f32[128,64,64]{0,2,1:T(8,128)}, u32[]{:S(2)}) copy-start(f32[128,64,64]{0,2,1:T(8,128)} %param.6) | copy-start | bytes 6291460
  6.4 33.0 %copy-start.2 = (f32[32,24]{1,0:T(8,128)S(1)}, f32[32,24]{1,0:T(8,128)}, u32[]{:S(2)}) copy-start(f32[32,24]{1,0:T(8,128)} %constant.17.clone.scalars) | copy-start | bytes 9220
  6.4 42.2 %collective-permute-start = (f32[1024,128]{1,0:T(8,128)S(1)}, f32[1024,128]{1,0:T(8,128)S(1)}, u32[]{:S(2)}, u32[]{:S(2)}) collective-permute-start(f32[1024,128]{1,0:T(8,128)S(1)} %get-tuple-element.14), channel_id=1, source_target_pairs={{16,48},{17,49},{18,50},{19,51},{20,52},{21,53},{22,54},{23,55},{2... | collective-permute-start | bytes 1572872 | tf_op jit(solution)/shard_map/ppermute | solution.py:443
  31.0 17.5 %all-to-all-start.1 = ((f32[32,16,128]{2,1,0:T(8,128)}), f32[32,16,128]{2,1,0:T(8,128)S(1)}, u32[]{:S(2)}, u32[]{:S(2)}) async-start(f32[32,16,128]{2,1,0:T(8,128)} %mix_moments.2), calls=%async_computation.1 | async-start | bytes 524288 | tf_op jit(solution)/shard_map/all_to_all | solution.py:175
  60.9 34.2 %collective-permute-start.1 = (f32[128,8,128]{2,1,0:T(8,128)S(1)}, f32[128,8,128]{2,1,0:T(8,128)S(1)}, u32[]{:S(2)}, u32[]{:S(2)}) collective-permute-start(f32[128,8,128]{2,1,0:T(8,128)S(1)} %get-tuple-element.17), channel_id=1, source_target_pairs={{16,48},{17,49},{18,50},{19,51},{20,52},{21,53},{22,54},{23,55},{2... | collective-permute-start | bytes 1572872 | tf_op jit(solution)/shard_map/ppermute | solution.py:447

commit v2 on v1

v2 whole, which is shorter than its diff:
```python
import functools

import jax
import jax.numpy as jnp
import numpy as np
from jax import lax
from jax.experimental import pallas as pl
from jax.experimental.pallas import tpu as pltpu
from jax.sharding import PartitionSpec as P

NV1 = 16
COUPLING = 0.25
LID_SPEED = 0.6
STEP = 6.0 / NV1
CENTRE = 0.5 * (NV1 - 1)
VEL = 32
LOCAL_Y = 8
HIGH = [float(np.sqrt(k + 0.5)) for k in range(4)]
HIGHEST = lax.Precision.HIGHEST
F32 = jnp.float32
BF16 = jnp.bfloat16
HALF = 64


def grid_speed(index):
    return (np.asarray(index, np.float64) - CENTRE) * STEP


def local_polynomials(y, z):
    r2 = y * y + z * z
    return [np.ones_like(r2), y, z, y * y, z * z, y * z, r2 * y, r2 * z]


def combination(x):
    c = np.zeros((13, 8))
    c[0, 0] = 1.0
    c[1, 0] = x
    c[2, 1] = 1.0
    c[3, 2] = 1.0
    c[4, 0] = x * x - 1.0
    c[5, 3], c[5, 0] = 1.0, -1.0
    c[6, 4], c[6, 0] = 1.0, -1.0
    c[7, 1] = x
    c[8, 2] = x
    c[9, 5] = 1.0
    c[10, 0], c[10, 3], c[10, 4] = x * (x * x - 5.0), x, x
    c[11, 1], c[11, 6] = x * x - 5.0, 1.0
    c[12, 2], c[12, 7] = x * x - 5.0, 1.0
    return c


def tables():
    speed = grid_speed(np.arange(NV1))
    weight = np.exp(-0.5 * speed * speed)
    total = weight.sum()
    weight = weight / total
    x, y, z = np.meshgrid(speed, speed, speed, indexing="ij")
    w = weight[:, None, None] * weight[None, :, None] * weight[None, None, :]
    g = np.stack(local_polynomials(y, z))
    per_x = np.stack([combination(s) for s in speed])
    h = np.einsum("xkj,jxyz->kxyz", per_x, g)
    norm = (w * h * h).sum(axis=(1, 2, 3))
    source = np.repeat(per_x * weight[:, None, None], 2, axis=0)
    target = np.repeat(per_x, 2, axis=0)
    mix = np.einsum("tkj,k,ski->tjsi", target, 1.0 / norm, source).reshape(VEL * 8, VEL * 8)
    return mix.astype(np.float32), speed, weight, float(total)


MIX, SPEED, WEIGHT, TOTAL = tables()


def split(a):
    hi = a.astype(BF16)
    return hi, (a - hi.astype(F32)).astype(BF16)


def lane_index(shape):
    return lax.broadcasted_iota(jnp.int32, shape, len(shape) - 1)


def row_index(shape):
    return lax.broadcasted_iota(jnp.int32, shape, len(shape) - 2)


class Place:
    def __init__(self, slabs):
        vel, slab = lax.axis_index("vel"), lax.axis_index("sp")
        self.vx = (vel // 2).astype(F32) * STEP - CENTRE * STEP
        self.sign_x = jnp.where(vel >= VEL // 2, 1.0, -1.0)
        self.scale_x = COUPLING * jnp.abs(self.vx)
        self.first_y = vel % 2 * LOCAL_Y
        self.sign_y = jnp.where(vel % 2 == 1, 1.0, -1.0)
        boundary = jnp.where(vel >= VEL // 2, 0, slabs - 1)
        self.wall_x = jnp.where(slab == boundary, 2.0, 0.0)

    def speed_y(self, step):
        return (self.first_y + step).astype(F32) * STEP - CENTRE * STEP


def outgoing_mask(lane, sign):
    return jnp.where(sign > 0, lane, 2 * HALF - 1 - lane) >= HALF


def trace_face(sign):
    return [HIGH[k] if k % 2 == 0 else HIGH[k] * sign for k in range(4)]


def lift_faces(sign):
    return [HIGH[k] if k % 2 == 0 else -HIGH[k] * sign for k in range(4)]


def kept(*shape, dtype=F32):
    return pltpu.VMEM(shape, dtype)


def here(x):
    return pltpu.with_memory_space_constraint(x, pltpu.VMEM)


def away(x):
    return pltpu.with_memory_space_constraint(x, pltpu.HBM)


def velocity_block(ref, step):
    return ref.at[pl.ds(pl.multiple_of(step * 16, 16), 16)]


def mode_block(ref, step):
    return ref.at[:, pl.ds(pl.multiple_of(step * 16, 16), 16), :]


def stream(pairs):
    def copies(step):
        return [pltpu.make_async_copy(source(step), target(step), sems.at[step]) for source, target, sems in pairs]

    def start(step):
        for copy in copies(step):
            copy.start()

    def wait(step):
        for copy in copies(step):
            copy.wait()

    return start, wait


AHEAD = 8


def start_first(start):
    for step in range(AHEAD):
        start(step)


def start_later(start, step):
    @pl.when(step + AHEAD < 8)
    def _():
        start(step + AHEAD)


BLOCKS_V = pltpu.VMEM((128, 64, 128), F32)
BLOCKS_Q = pltpu.VMEM((8, 64, 16, 128), F32)
SEMS = pltpu.SemaphoreType.DMA((8,))


VMEM = pl.BlockSpec(memory_space=pltpu.VMEM)
HBM = pl.BlockSpec(memory_space=pltpu.HBM)
PARAMS = pltpu.CompilerParams(vmem_limit_bytes=24 * 2**20)


def moment_weights(first_y):
    lane, row = lane_index((8, 128)), row_index((8, 128))
    y = (lane // 16 + first_y).astype(F32) * STEP - CENTRE * STEP
    z = (lane % 16).astype(F32) * STEP - CENTRE * STEP
    r2 = y * y + z * z
    polynomial = jnp.ones((8, 128), F32)
    for j, g in enumerate([y, z, y * y, z * z, y * z, r2 * y, r2 * z]):
        polynomial = jnp.where(row == j + 1, g, polynomial)
    hi, lo = split(polynomial * jnp.exp(-0.5 * r2) * (1.0 / (TOTAL * TOTAL)))
    half = jnp.concatenate([hi.astype(F32), lo.astype(F32)], axis=0).astype(BF16)
    return jnp.concatenate([half, half], axis=1)


def first_moments_kernel(prior, moments, cells, arrived):
    copies = []
    for step in range(8):
        part = pl.ds(step * 8, 8)
        copies.append(pltpu.make_async_copy(prior.at[part], cells.at[part], arrived.at[step]))
        copies[-1].start()
    weights = moment_weights(lax.axis_index("vel") % 2 * LOCAL_Y)
    for step in range(8):
        copies[step].wait()
        for q in range(step * 8, step * 8 + 8):
            hi, lo = split(cells[q])
            both = jnp.concatenate([hi, lo], axis=0)
            product = jnp.dot(weights, both, preferred_element_type=F32)
            moments[q] = product[:8] + product[8:]


def first_moments(prior):
    return pl.pallas_call(
        first_moments_kernel,
        in_specs=[HBM],
        out_specs=VMEM,
        out_shape=kept(64, 8, 128),
        scratch_shapes=[pltpu.VMEM((64, 128, 128), F32), SEMS],
        compiler_params=PARAMS,
        name="first_moments",
    )(away(prior)).reshape(VEL, 16, 128)


def pack_kernel(inverse, packed, rows, blocks, arrived):
    fetch, wait = stream([(lambda i: inverse.at[pl.ds(i * 8, 8)], lambda i: blocks.at[pl.ds(i * 8, 8)], arrived)])
    for step in range(8):
        fetch(step)
    for step in range(8):
        wait(step)
        for p in range(step * 8, step * 8 + 8):
            hi, lo = split(blocks[p])
            both = jnp.concatenate([hi.astype(F32), lo.astype(F32)], axis=0)
            rows[pl.ds(p, 128, stride=PITCH), :] = both.T

    def step(v, carry):
        packed[v] = rows[pl.ds(pl.multiple_of(v * PITCH, 8), 64), :].astype(BF16)
        return carry

    lax.fori_loop(0, 128, step, 0, unroll=8)


PITCH = 72


def pack(inverse):
    return pl.pallas_call(
        pack_kernel,
        in_specs=[HBM],
        out_specs=VMEM,
        out_shape=kept(128, 64, 128, dtype=BF16),
        scratch_shapes=[pltpu.VMEM((128 * PITCH, 128), F32), pltpu.VMEM((64, 64, 128), F32), SEMS],
        compiler_params=PARAMS,
        name="pack",
    )(away(jnp.transpose(inverse, (1, 2, 0))))


def mix_kernel(mix, gathered, mixed):
    part = jnp.concatenate([gathered[:, low * 8 : low * 8 + 8, :].reshape(VEL * 8, 128) for low in range(2)], axis=1)
    result = jnp.dot(mix[...], part, preferred_element_type=F32, precision=HIGHEST)
    for low in range(2):
        mixed[:, low * 8 : low * 8 + 8, :] = result[:, low * 128 : low * 128 + 128].reshape(VEL, 8, 128)


def mix_moments(mix, gathered):
    return pl.pallas_call(
        mix_kernel,
        in_specs=[VMEM, VMEM],
        out_specs=VMEM,
        out_shape=kept(VEL, 16, 128),
        compiler_params=PARAMS,
        name="mix_moments",
    )(here(mix), here(gathered))


def sum_over_velocities(mix, partial_sums, beside):
    gathered = lax.all_to_all(partial_sums, "vel", 0, 0)
    gathered, beside = lax.optimization_barrier((gathered, beside))
    mixed = mix_moments(mix, gathered)
    mixed, beside = lax.optimization_barrier((mixed, beside))
    return lax.all_to_all(mixed, "vel", 0, 0).reshape(512, 128), beside


def add_inflow(source, base, target, send, place, step, mask):
    y = place.speed_y(step)
    lane, row = lane_index((8, 128)), row_index((8, 128))
    trace_x, lift_x = trace_face(place.sign_x), lift_faces(place.sign_x)
    trace_y, lift_y = trace_face(place.sign_y), lift_faces(place.sign_y)
    up_y = place.sign_y > 0
    shift_y = jnp.where(up_y, 8, 120)
    cell_y = jnp.where(up_y, lane // 8 % 8, 7 - lane // 8 % 8)
    scale_y = jnp.where(cell_y > 0, COUPLING * jnp.abs(y), 0.0)
    wall_y = jnp.where(cell_y > 0, 0.0, 2.0 * COUPLING * jnp.abs(y))
    scale_x = jnp.where(mask, place.scale_x, 0.0)
    wall_x = jnp.where(mask, 0.0, place.wall_x * place.scale_x)
    lid = 2.0 * jnp.exp(jnp.full((8, 128), LID_SPEED, F32) * place.vx - 0.5 * LID_SPEED * LID_SPEED)
    for part in range(2):
        up = part == 1
        speed = jnp.abs((row + (part * 8)).astype(F32) - CENTRE) * (STEP * COUPLING)
        inside = (lane % 8 > 0) if up else (lane % 8 < 7)
        scale_z = jnp.where(inside, speed, 0.0)
        wall_z = jnp.where(inside, 0.0, speed * (2.0 if up else lid))
        trace_z, lift_z = trace_face(1.0 if up else -1.0), lift_faces(1.0 if up else -1.0)
        rows = pl.ds(pl.multiple_of(step * 16 + part * 8, 8), 8)
        face_x = [None] * 16
        for low in range(8):
            pair = []
            for r in (low, low + 8):
                trace = sum(trace_x[p0] * source(part, p0 * 16 + r) for p0 in range(4))
                turned = pltpu.roll(trace, HALF, 1)
                pair.append((trace, turned))
                face_x[r] = turned * scale_x
            send[low, rows, :] = jnp.where(mask, pair[1][0], pair[0][1])
        face_x[0] = face_x[0] + wall_x
        for p0 in range(4):
            x = [[source(part, p0 * 16 + p1 * 4 + p2) for p2 in range(4)] for p1 in range(4)]
            face_y, face_z = [], []
            for k in range(4):
                ty = sum(trace_y[p1] * x[p1][k] for p1 in range(4))
                ty = pltpu.roll(ty, shift_y, 1) * scale_y
                tz = sum(trace_z[p2] * x[k][p2] for p2 in range(4))
                tz = pltpu.roll(tz, 1 if up else 127, 1) * scale_z
                if p0 == 0 and k == 0:
                    ty = ty + wall_y
                    tz = tz + wall_z
                face_y.append(ty)
                face_z.append(tz)
            for p1 in range(4):
                for p2 in range(4):
                    q, r = p0 * 16 + p1 * 4 + p2, p1 * 4 + p2
                    value = base(part, q) + lift_x[p0] * face_x[r] + lift_y[p1] * face_y[p2] + lift_z[p2] * face_z[p1]
                    target[part * 512 + q * 8 : part * 512 + q * 8 + 8, :] = value


def velocity_rows(v):
    return pl.ds(v // 8 * 512 + v % 8, 64, stride=8)


def block_reader(ref):
    def read(part, q):
        return ref[q, part * 8 : part * 8 + 8, :]

    return read


def row_reader(ref):
    def read(part, q):
        return ref[part * 512 + q * 8 : part * 512 + q * 8 + 8, :]

    return read


def prepare_kernel(slabs, prior, right, send, scratch, cells, made, arrived, sent):
    place = Place(slabs)
    mask = outgoing_mask(lane_index((8, 128)), place.sign_x)
    fetch, wait = stream([(lambda i: mode_block(prior, i), lambda i: cells.at[i], arrived)])
    put, finish = stream([(lambda i: velocity_block(made, i), lambda i: velocity_block(right, i), sent)])
    start_first(fetch)

    def loop(step, carry):
        wait(step)
        start_later(fetch, step)
        read = block_reader(cells.at[step])
        add_inflow(read, read, scratch, send, place, step, mask)
        for v in range(16):
            made[step * 16 + v] = scratch[velocity_rows(v), :]
        put(step)
        return carry

    lax.fori_loop(0, 8, loop, 0)
    for step in range(8):
        finish(step)


def prepare(slabs, prior):
    return pl.pallas_call(
        functools.partial(prepare_kernel, slabs),
        in_specs=[HBM],
        out_specs=[HBM, VMEM],
        out_shape=[pltpu.HBM((128, 64, 128), F32), kept(8, 128, 128)],
        scratch_shapes=[pltpu.VMEM((1024, 128), F32), BLOCKS_Q, BLOCKS_V, SEMS, SEMS],
        compiler_params=PARAMS,
        name="prepare",
    )(away(prior))


def prepare_next_kernel(
    slabs, fresh, prior, right, send, rows, scratch, columns, cells, made, arrived, arrived_prior, sent
):
    place = Place(slabs)
    mask = outgoing_mask(lane_index((8, 128)), place.sign_x)
    fetch, wait = stream(
        [
            (lambda i: velocity_block(fresh, i), lambda i: velocity_block(columns, i), arrived),
            (lambda i: mode_block(prior, i), lambda i: cells.at[i], arrived_prior),
        ]
    )
    put, finish = stream([(lambda i: velocity_block(made, i), lambda i: velocity_block(right, i), sent)])
    start_first(fetch)

    def loop(step, carry):
        wait(step)
        start_later(fetch, step)
        for v in range(16):
            rows[velocity_rows(v), :] = columns[step * 16 + v]
        add_inflow(row_reader(rows), block_reader(cells.at[step]), scratch, send, place, step, mask)
        for v in range(16):
            made[step * 16 + v] = scratch[velocity_rows(v), :]
        put(step)
        return carry

    lax.fori_loop(0, 8, loop, 0)
    for step in range(8):
        finish(step)


def prepare_next(slabs, fresh, prior):
    return pl.pallas_call(
        functools.partial(prepare_next_kernel, slabs),
        in_specs=[HBM, HBM],
        out_specs=[HBM, VMEM],
        out_shape=[pltpu.HBM((128, 64, 128), F32), kept(8, 128, 128)],
        scratch_shapes=[
            pltpu.VMEM((1024, 128), F32),
            pltpu.VMEM((1024, 128), F32),
            BLOCKS_V,
            BLOCKS_Q,
            BLOCKS_V,
            SEMS,
            SEMS,
            SEMS,
        ],
        compiler_params=PARAMS,
        name="prepare_next",
    )(away(fresh), away(prior))


def split_planes(mixed, planes):
    for j in range(8):
        planes[j] = mixed[pl.ds(j, 64, stride=8), :]


def relax(place, step, right, packed, recv, planes, columns, mask, store):
    y = place.speed_y(step)
    columns[0] = planes[0] + y * (planes[1] + y * (planes[3] + y * planes[6]))
    columns[1] = planes[2] + y * (planes[5] + y * planes[7])
    columns[2] = planes[4] + y * planes[6]
    columns[3] = planes[7]
    lift = lift_faces(place.sign_x)
    for low in range(8):
        z = float(SPEED[15 - low])
        even = columns[0] + (z * z) * columns[2]
        odd = z * columns[1] + (z * z * z) * columns[3]
        for v, equilibrium in ((low, even - odd), (15 - low, even + odd)):
            at = step * 16 + v
            edge = recv[pl.ds(at, 8, stride=128), :]
            both = jnp.concatenate([edge, pltpu.roll(edge, HALF, 1)], axis=0)
            both = jnp.where(mask, 0.0, both) * place.scale_x
            inflow = jnp.concatenate([lift[p0] * both for p0 in range(4)], axis=0)
            hi, lo = split(right[at] + equilibrium + inflow)
            block = packed[at]
            fresh = jnp.dot(
                jnp.concatenate([block, block], axis=1),
                jnp.concatenate([hi, hi, lo, lo], axis=0),
                preferred_element_type=F32,
            )
            store(v, fresh)


def middle_kernel(
    slabs, right_away, packed, recv, mixed, fresh_away, moments, planes, columns, sums, right, fresh, arrived, sent
):
    place = Place(slabs)
    mask = outgoing_mask(lane_index((16, 128)), place.sign_x)
    fetch, wait = stream([(lambda i: velocity_block(right_away, i), lambda i: velocity_block(right, i), arrived)])
    put, finish = stream([(lambda i: velocity_block(fresh, i), lambda i: velocity_block(fresh_away, i), sent)])
    start_first(fetch)
    split_planes(mixed, planes)
    sums[...] = jnp.zeros_like(sums)

    def loop(step, carry):
        def store(v, column):
            fresh[step * 16 + v] = column

        wait(step)
        start_later(fetch, step)
        relax(place, step, right, packed, recv, planes, columns, mask, store)
        put(step)
        y = place.speed_y(step)
        weight = jnp.exp(jnp.full((64, 128), -0.5, F32) * (y * y)) * (1.0 / TOTAL)
        s = [None] * 4
        for low in range(8):
            z, w = float(SPEED[15 - low]), float(WEIGHT[low])
            minus, plus = fresh[step * 16 + low], fresh[step * 16 + 15 - low]
            terms = [w * (plus + minus), (w * z) * (plus - minus)]
            for k in range(4):
                term = terms[k % 2] if k < 2 else (z * z) * terms[k % 2]
                s[k] = term if s[k] is None else s[k] + term
        s = [weight * part for part in s]
        y2 = y * y
        totals = [s[0], y * s[0], s[1], y2 * s[0], s[2], y * s[1], y * (y2 * s[0] + s[2]), s[3] + y2 * s[1]]
        for j in range(8):
            sums[j] = sums[j] + totals[j]
        return carry

    lax.fori_loop(0, 8, loop, 0)
    for j in range(8):
        moments[pl.ds(j, 64, stride=8), :] = sums[j]
    for step in range(8):
        finish(step)


def middle(slabs, right, packed, recv, mixed):
    fresh, moments = pl.pallas_call(
        functools.partial(middle_kernel, slabs),
        in_specs=[HBM, VMEM, VMEM, VMEM],
        out_specs=[HBM, VMEM],
        out_shape=[pltpu.HBM((128, 64, 128), F32), kept(512, 128)],
        scratch_shapes=[
            pltpu.VMEM((8, 64, 128), F32),
            pltpu.VMEM((4, 64, 128), F32),
            pltpu.VMEM((8, 64, 128), F32),
            BLOCKS_V,
            BLOCKS_V,
            SEMS,
            SEMS,
        ],
        compiler_params=PARAMS,
        name="middle",
    )(away(right), here(packed), here(recv), here(mixed))
    return fresh, moments.reshape(VEL, 16, 128)


def last_kernel(slabs, right_away, packed, recv, mixed, out, planes, columns, right, blocks, arrived, sent):
    place = Place(slabs)
    mask = outgoing_mask(lane_index((16, 128)), place.sign_x)
    fetch, wait = stream([(lambda i: velocity_block(right_away, i), lambda i: velocity_block(right, i), arrived)])
    put, finish = stream([(lambda i: blocks.at[i], lambda i: mode_block(out, i), sent)])
    start_first(fetch)
    split_planes(mixed, planes)

    def loop(step, carry):
        flat = blocks.at[step].reshape(1024, 128)

        def store(v, fresh):
            flat[pl.ds(v, 64, stride=16), :] = fresh

        wait(step)
        start_later(fetch, step)
        relax(place, step, right, packed, recv, planes, columns, mask, store)
        put(step)
        return carry

    lax.fori_loop(0, 8, loop, 0)
    for step in range(8):
        finish(step)


def last(slabs, right, packed, recv, mixed):
    return pl.pallas_call(
        functools.partial(last_kernel, slabs),
        in_specs=[HBM, VMEM, VMEM, VMEM],
        out_specs=HBM,
        out_shape=pltpu.HBM((64, 128, 128), F32),
        scratch_shapes=[
            pltpu.VMEM((8, 64, 128), F32),
            pltpu.VMEM((4, 64, 128), F32),
            BLOCKS_V,
            BLOCKS_Q,
            SEMS,
            SEMS,
        ],
        compiler_params=PARAMS,
        name="last",
    )(away(right), here(packed), here(recv), here(mixed))


def halo_pairs(slabs):
    pairs = []
    for slab in range(slabs):
        for vel in range(VEL):
            other = slab + 1 if vel >= VEL // 2 else slab - 1
            if 0 <= other < slabs:
                pairs.append((slab * VEL + vel, other * VEL + vel))
    return pairs


def body(slabs, prior, block_inverse):
    mix = jnp.asarray(MIX)
    axes = ("sp", "vel")
    pairs = halo_pairs(slabs)
    cells = prior.reshape(64, 128, 128)
    moments = first_moments(cells)
    mixed, (right, send) = sum_over_velocities(mix, moments, prepare(slabs, cells))
    recv = lax.ppermute(send, axes, pairs).reshape(1024, 128)
    packed = pack(block_inverse)
    fresh, moments = middle(slabs, right, packed, recv, mixed)
    mixed, (right, send) = sum_over_velocities(mix, moments, prepare_next(slabs, fresh, cells))
    recv = lax.ppermute(send, axes, pairs).reshape(1024, 128)
    return last(slabs, right, packed, recv, mixed).reshape(prior.shape)


def solution(mesh):
    spec = P(None, None, None, "vel", "sp")
    return jax.shard_map(
        functools.partial(body, mesh.shape["sp"]),
        mesh=mesh,
        in_specs=(spec, P("vel", None, None)),
        out_specs=spec,
        check_vma=False,
    )
```

time: 105 us -> 82.9 us (0.79); the launches traced: 103 us -> 82.4 us
  blocking collectives: 48.9 us -> 14.9 us
  starting transfers between devices: 9.11 us -> 26.2 us
  waiting for transfers between devices: 0.01 us -> 11.6 us
  local copies, waits for them, and re-layouts: 8.11 us -> 0.01 us
  Pallas kernels: 37.1 us -> 29.7 us
    all_to_all x3 -> x1, blocking collectives: 48.9 us -> 14.9 us  [sum_over_velocities(): return (lax.all_to_all(mixed, 'vel', 0, 0).reshape(512, 128), beside)]
    all_to_all x1 -> x3, starting transfers between devices: 3.87 us -> 20.2 us  [the longest x2 14.3 us: sum_over_velocities(): gathered = lax.all_to_all(partial_sums, 'vel', 0, 0)]
    all_to_all x1 -> x3, waiting for transfers between devices: 0.01 us -> 11.6 us  [the longest x2 5.98 us: sum_over_velocities(): gathered = lax.all_to_all(partial_sums, 'vel', 0, 0)]
    unnamed x11 -> x2, local copies, waits for them, and re-layouts: 8.11 us -> 0.01 us
    pallas_call x6 -> x8, Pallas kernels: 37.1 us -> 29.7 us  [the longest x1 6.02 us: middle(): pl.pallas_call(functools.partial(middle_kernel, slabs), in_specs=[HBM, VM...]
  transfers between devices with their start and end apart: 3 -> 5, of which waited for: 0 -> 3; matrix products, arithmetic and copies ran while one was open for 4% -> 0% of each run, Pallas kernels for 13% -> 16%
where the time goes in v2:
time: 82.9 us; the launch traced here: 82.4 us
  Pallas kernels  29.7 us (36%)
  starting transfers between devices  26.2 us (32%)
  blocking collectives  14.9 us (18%)
  waiting for transfers between devices  11.6 us (14%)
    all_to_all x1, blocking collectives, sum_over_velocities(): return (lax.all_to_all(mixed, 'vel', 0, 0).reshape(512, 128), beside)  14.9 us
    all_to_all x2, starting transfers between devices, sum_over_velocities(): gathered = lax.all_to_all(partial_sums, 'vel', 0, 0)  14.3 us
    pallas_call x1, Pallas kernels, middle(): pl.pallas_call(functools.partial(middle_kernel, slabs), in_specs=[HBM, VM...  6.02 us
    ppermute x2, starting transfers between devices, body(): recv = lax.ppermute(send, axes, pairs).reshape(1024, 128)  5.98 us
    all_to_all x2, waiting for transfers between devices, sum_over_velocities(): gathered = lax.all_to_all(partial_sums, 'vel', 0, 0)  5.98 us
    all_to_all x1, starting transfers between devices, sum_over_velocities(): return (lax.all_to_all(mixed, 'vel', 0, 0).reshape(512, 128), beside)  5.91 us
    pallas_call x1, Pallas kernels, prepare_next(): pl.pallas_call(functools.partial(prepare_next_kernel, slabs), in_specs=[H...  5.8 us
    all_to_all x1, waiting for transfers between devices, sum_over_velocities(): return (lax.all_to_all(mixed, 'vel', 0, 0).reshape(512, 128), beside)  5.58 us
  transfers between devices with their start and end apart: 5, of which 3 were waited for; matrix products, arithmetic and copies ran while one was open for 0% of the time, Pallas kernels for 16%

profile of v2, /device:TPU:1, one launch (start us, length us, event | category | flops | bytes accessed | tf_op | source)
XLA Modules:
  0.0 82.4 jit_solution(8517100654223890814)
XLA Ops:
  0.0 0.0 copy-start
  0.0 3.4 %first_moments.1 = f32[64,8,128]{2,1,0:T(8,128)} custom-call(f32[64,128,128]{2,1,0:T(8,128)} %bitcast.13), custom_call_target="tpu_custom_call" | custom-call | tf_op jit(solution)/shard_map/first_moments/pallas_call | solution.py:201
  3.4 9.8 %all-to-all-start = ((f32[32,16,128]{2,1,0:T(8,128)}), f32[32,16,128]{2,1,0:T(8,128)S(1)}, u32[]{:S(2)}, u32[]{:S(2)}) async-start(f32[32,16,128]{2,1,0:T(8,128)} %bitcast.1), calls=%async_computation | async-start | bytes 524288 | tf_op jit(solution)/shard_map/all_to_all | solution.py:264
  13.2 5.2 %prepare.1 = (f32[128,64,128]{2,1,0:T(8,128)}, f32[8,128,128]{2,1,0:T(8,128)}) custom-call(f32[64,128,128]{2,1,0:T(8,128)} %bitcast.14), custom_call_target="tpu_custom_call" | custom-call | tf_op jit(solution)/shard_map/prepare/pallas_call | solution.py:363
  18.5 2.8 %all-to-all-done.gathered = f32[32,16,128]{2,1,0:T(8,128)S(1)} async-done(((f32[32,16,128]{2,1,0:T(8,128)}), f32[32,16,128]{2,1,0:T(8,128)S(1)}, u32[]{:S(2)}, u32[]{:S(2)}) %all-to-all-start) | async-done | bytes 262176 | tf_op jit(solution)/shard_map/all_to_all | solution.py:264
  21.3 0.0 copy-done
  21.3 1.1 %mix_moments.2 = f32[32,16,128]{2,1,0:T(8,128)} custom-call(f32[256,256]{1,0:T(8,128)S(1)} %copy-done, f32[32,16,128]{2,1,0:T(8,128)S(1)} %all-to-all-done.gathered), custom_call_target="tpu_custom_call" | custom-call | tf_op jit(solution)/shard_map/mix_moments/pallas_call | solution.py:253
  22.4 3.9 %collective-permute-start = (f32[8,128,128]{2,1,0:T(8,128)}, f32[8,128,128]{2,1,0:T(8,128)S(1)}, u32[]{:S(2)}, u32[]{:S(2)}) collective-permute-start(f32[8,128,128]{2,1,0:T(8,128)} %get-tuple-element.29), channel_id=1, source_target_pairs={{16,48},{17,49},{18,50},{19,51},{20,52},{21,53},{22,54},{23,55},{2... | collective-permute-start | bytes 1572872 | tf_op jit(solution)/shard_map/ppermute | solution.py:582
  26.3 5.9 %all-to-all-start.1 = ((f32[32,16,128]{2,1,0:T(8,128)}), f32[32,16,128]{2,1,0:T(8,128)S(1)}, u32[]{:S(2)}, u32[]{:S(2)}) async-start(f32[32,16,128]{2,1,0:T(8,128)} %mix_moments.2), calls=%async_computation.1 | async-start | bytes 524288 | tf_op jit(solution)/shard_map/all_to_all | solution.py:268
  32.2 2.4 %pack.1.packed = bf16[128,64,128]{2,1,0:T(8,128)(2,1)S(1)} custom-call(f32[64,64,128]{2,1,0:T(8,128)} %bitcast.16), custom_call_target="tpu_custom_call" | custom-call | tf_op jit(solution)/shard_map/pack/pallas_call | solution.py:234
  34.6 5.6 %all-to-all-done.1 = f32[32,16,128]{2,1,0:T(8,128)S(1)} async-done(((f32[32,16,128]{2,1,0:T(8,128)}), f32[32,16,128]{2,1,0:T(8,128)S(1)}, u32[]{:S(2)}, u32[]{:S(2)}) %all-to-all-start.1) | async-done | bytes 262176 | tf_op jit(solution)/shard_map/all_to_all | solution.py:268
  40.2 0.0 collective-permute-done
  40.2 6.0 %middle.1 = (f32[128,64,128]{2,1,0:T(8,128)}, f32[512,128]{1,0:T(8,128)}) custom-call(f32[128,64,128]{2,1,0:T(8,128)} %get-tuple-element.28.right_away, bf16[128,64,128]{2,1,0:T(8,128)(2,1)S(1)} %pack.1.packed, f32[1024,128]{1,0:T(8,128)S(1)} %bitcast.11, f32[512,128]{1,0:T(8,128)S(1)} %bitcast.9), custom_call_target="tpu_custom_call" | custom-call | tf_op jit(solution)/shard_map/middle/pallas_call | solution.py:501
  46.2 4.4 %all-to-all-start.2 = ((f32[32,16,128]{2,1,0:T(8,128)}), f32[32,16,128]{2,1,0:T(8,128)S(1)}, u32[]{:S(2)}, u32[]{:S(2)}) async-start(f32[32,16,128]{2,1,0:T(8,128)} %bitcast.5), calls=%async_computation.2 | async-start | bytes 524288 | tf_op jit(solution)/shard_map/all_to_all | solution.py:264
  50.7 5.8 %prepare_next.1 = (f32[128,64,128]{2,1,0:T(8,128)}, f32[8,128,128]{2,1,0:T(8,128)S(1)}) custom-call(f32[128,64,128]{2,1,0:T(8,128)} %get-tuple-element.32.fresh, f32[64,128,128]{2,1,0:T(8,128)} %bitcast.15), custom_call_target="tpu_custom_call" | custom-call | tf_op jit(solution)/shard_map/prepare_next/pallas_call | solution.py:405
  56.5 3.1 %all-to-all-done.2.gathered = f32[32,16,128]{2,1,0:T(8,128)S(1)} async-done(((f32[32,16,128]{2,1,0:T(8,128)}), f32[32,16,128]{2,1,0:T(8,128)S(1)}, u32[]{:S(2)}, u32[]{:S(2)}) %all-to-all-start.2) | async-done | bytes 262176 | tf_op jit(solution)/shard_map/all_to_all | solution.py:264
  59.7 0.4 mix_moments.3
  60.0 2.1 %collective-permute-start.1 = (f32[8,128,128]{2,1,0:T(8,128)S(1)}, f32[8,128,128]{2,1,0:T(8,128)S(1)}, u32[]{:S(2)}, u32[]{:S(2)}) collective-permute-start(f32[8,128,128]{2,1,0:T(8,128)S(1)} %get-tuple-element.39), channel_id=1, source_target_pairs={{16,48},{17,49},{18,50},{19,51},{20,52},{21,53},{22,54},{23,55},{2... | collective-permute-start | bytes 1572872 | tf_op jit(solution)/shard_map/ppermute | solution.py:586
  62.1 14.9 %all_to_all.20 = f32[32,16,128]{2,1,0:T(8,128)S(1)} all-to-all(f32[32,16,128]{2,1,0:T(8,128)S(1)} %mix_moments.3), channel_id=1, replica_groups=mesh['sp'=4,'vel'=32] {'vel'}, dimensions={0} | all-to-all | bytes 524288 | tf_op jit(solution)/shard_map/all_to_all | solution.py:268
  77.1 0.0 collective-permute-done.1
  77.1 5.4 %last.1 = f32[64,128,128]{2,1,0:T(8,128)} custom-call(f32[128,64,128]{2,1,0:T(8,128)} %get-tuple-element.38.right_away, bf16[128,64,128]{2,1,0:T(8,128)(2,1)S(1)} %pack.1.packed, f32[1024,128]{1,0:T(8,128)S(1)} %bitcast.12, f32[512,128]{1,0:T(8,128)S(1)} %bitcast.10), custom_call_target="tpu_custom_call" | custom-call | tf_op jit(solution)/shard_map/last/pallas_call | solution.py:547
Async XLA Ops:
  0.0 21.3 %copy-start = (f32[256,256]{1,0:T(8,128)S(1)}, f32[256,256]{1,0:T(8,128)}, u32[]{:S(2)}) copy-start(f32[256,256]{1,0:T(8,128)} %constant.2.clone.mix) | copy-start | bytes 786436
  3.4 17.9 %all-to-all-start = ((f32[32,16,128]{2,1,0:T(8,128)}), f32[32,16,128]{2,1,0:T(8,128)S(1)}, u32[]{:S(2)}, u32[]{:S(2)}) async-start(f32[32,16,128]{2,1,0:T(8,128)} %bitcast.1), calls=%async_computation | async-start | bytes 524288 | tf_op jit(solution)/shard_map/all_to_all | solution.py:264
  22.4 17.8 %collective-permute-start = (f32[8,128,128]{2,1,0:T(8,128)}, f32[8,128,128]{2,1,0:T(8,128)S(1)}, u32[]{:S(2)}, u32[]{:S(2)}) collective-permute-start(f32[8,128,128]{2,1,0:T(8,128)} %get-tuple-element.29), channel_id=1, source_target_pairs={{16,48},{17,49},{18,50},{19,51},{20,52},{21,53},{22,54},{23,55},{2... | collective-permute-start | bytes 1572872 | tf_op jit(solution)/shard_map/ppermute | solution.py:582
  26.3 13.9 %all-to-all-start.1 = ((f32[32,16,128]{2,1,0:T(8,128)}), f32[32,16,128]{2,1,0:T(8,128)S(1)}, u32[]{:S(2)}, u32[]{:S(2)}) async-start(f32[32,16,128]{2,1,0:T(8,128)} %mix_moments.2), calls=%async_computation.1 | async-start | bytes 524288 | tf_op jit(solution)/shard_map/all_to_all | solution.py:268
  46.2 13.4 %all-to-all-start.2 = ((f32[32,16,128]{2,1,0:T(8,128)}), f32[32,16,128]{2,1,0:T(8,128)S(1)}, u32[]{:S(2)}, u32[]{:S(2)}) async-start(f32[32,16,128]{2,1,0:T(8,128)} %bitcast.5), calls=%async_computation.2 | async-start | bytes 524288 | tf_op jit(solution)/shard_map/all_to_all | solution.py:264
  60.0 17.0 %collective-permute-start.1 = (f32[8,128,128]{2,1,0:T(8,128)S(1)}, f32[8,128,128]{2,1,0:T(8,128)S(1)}, u32[]{:S(2)}, u32[]{:S(2)}) collective-permute-start(f32[8,128,128]{2,1,0:T(8,128)S(1)} %get-tuple-element.39), channel_id=1, source_target_pairs={{16,48},{17,49},{18,50},{19,51},{20,52},{21,53},{22,54},{23,55},{2... | collective-permute-start | bytes 1572872 | tf_op jit(solution)/shard_map/ppermute | solution.py:586

commit v3 on v2

--- a/solution.py
+++ b/solution.py
@@ -20,6 +20,14 @@
 F32 = jnp.float32
 BF16 = jnp.bfloat16
 HALF = 64
+
+
+def ring_hops(vel):
+    y, z = vel // 4 % 4, vel % 4
+    return vel // 16 + min(y, 4 - y) + min(z, 4 - z)
+
+
+ORDER = sorted(range(VEL), key=lambda vel: -ring_hops(vel))
 
 
 def grid_speed(index):
@@ -63,6 +71,7 @@
     source = np.repeat(per_x * weight[:, None, None], 2, axis=0)
     target = np.repeat(per_x, 2, axis=0)
     mix = np.einsum("tkj,k,ski->tjsi", target, 1.0 / norm, source).reshape(VEL * 8, VEL * 8)
+    mix = mix.reshape(VEL, 8, VEL, 8)[ORDER][:, :, ORDER].reshape(VEL * 8, VEL * 8)
     return mix.astype(np.float32), speed, weight, float(total)
 
 
@@ -144,18 +153,9 @@
     return start, wait
 
 
-AHEAD = 8
-
-
-def start_first(start):
-    for step in range(AHEAD):
+def start_all(start):
+    for step in range(8):
         start(step)
-
-
-def start_later(start, step):
-    @pl.when(step + AHEAD < 8)
-    def _():
-        start(step + AHEAD)
 
 
 BLOCKS_V = pltpu.VMEM((128, 64, 128), F32)
@@ -181,29 +181,32 @@
     return jnp.concatenate([half, half], axis=1)
 
 
-def first_moments_kernel(prior, moments, cells, arrived):
-    copies = []
-    for step in range(8):
-        part = pl.ds(step * 8, 8)
-        copies.append(pltpu.make_async_copy(prior.at[part], cells.at[part], arrived.at[step]))
-        copies[-1].start()
+def first_moments_kernel(prior, moments, cells, sums, arrived, sent):
+    def part(ref, step):
+        return ref.at[pl.ds(step * 8, 8)]
+
+    fetch, wait = stream([(lambda i: part(prior, i), lambda i: part(cells, i), arrived)])
+    put, finish = stream([(lambda i: part(sums, i), lambda i: part(moments, i), sent)])
+    start_all(fetch)
     weights = moment_weights(lax.axis_index("vel") % 2 * LOCAL_Y)
     for step in range(8):
-        copies[step].wait()
+        wait(step)
         for q in range(step * 8, step * 8 + 8):
             hi, lo = split(cells[q])
-            both = jnp.concatenate([hi, lo], axis=0)
-            product = jnp.dot(weights, both, preferred_element_type=F32)
-            moments[q] = product[:8] + product[8:]
+            product = jnp.dot(weights, jnp.concatenate([hi, lo], axis=0), preferred_element_type=F32)
+            sums[q] = product[:8] + product[8:]
+        put(step)
+    for step in range(8):
+        finish(step)
 
 
 def first_moments(prior):
     return pl.pallas_call(
         first_moments_kernel,
         in_specs=[HBM],
-        out_specs=VMEM,
-        out_shape=kept(64, 8, 128),
-        scratch_shapes=[pltpu.VMEM((64, 128, 128), F32), SEMS],
+        out_specs=HBM,
+        out_shape=pltpu.HBM((64, 8, 128), F32),
+        scratch_shapes=[pltpu.VMEM((64, 128, 128), F32), pltpu.VMEM((64, 8, 128), F32), SEMS, SEMS],
         compiler_params=PARAMS,
         name="first_moments",
     )(away(prior)).reshape(VEL, 16, 128)
@@ -261,11 +264,11 @@
 
 
 def sum_over_velocities(mix, partial_sums, beside):
-    gathered = lax.all_to_all(partial_sums, "vel", 0, 0)
+    gathered = lax.all_to_all(partial_sums, "vel", 0, 0, axis_index_groups=[ORDER])
     gathered, beside = lax.optimization_barrier((gathered, beside))
     mixed = mix_moments(mix, gathered)
     mixed, beside = lax.optimization_barrier((mixed, beside))
-    return lax.all_to_all(mixed, "vel", 0, 0).reshape(512, 128), beside
+    return lax.all_to_all(mixed, "vel", 0, 0, axis_index_groups=[ORDER]).reshape(512, 128), beside
 
 
 def add_inflow(source, base, target, send, place, step, mask):
@@ -342,11 +345,10 @@
     mask = outgoing_mask(lane_index((8, 128)), place.sign_x)
     fetch, wait = stream([(lambda i: mode_block(prior, i), lambda i: cells.at[i], arrived)])
     put, finish = stream([(lambda i: velocity_block(made, i), lambda i: velocity_block(right, i), sent)])
-    start_first(fetch)
+    start_all(fetch)
 
     def loop(step, carry):
         wait(step)
-        start_later(fetch, step)
         read = block_reader(cells.at[step])
         add_inflow(read, read, scratch, send, place, step, mask)
         for v in range(16):
@@ -383,11 +385,10 @@
         ]
     )
     put, finish = stream([(lambda i: velocity_block(made, i), lambda i: velocity_block(right, i), sent)])
-    start_first(fetch)
+    start_all(fetch)
 
     def loop(step, carry):
         wait(step)
-        start_later(fetch, step)
         for v in range(16):
             rows[velocity_rows(v), :] = columns[step * 16 + v]
         add_inflow(row_reader(rows), block_reader(cells.at[step]), scratch, send, place, step, mask)
@@ -433,7 +434,7 @@
     columns[1] = planes[2] + y * (planes[5] + y * planes[7])
     columns[2] = planes[4] + y * planes[6]
     columns[3] = planes[7]
-    lift = lift_faces(place.sign_x)
+    lift = [place.scale_x * face for face in lift_faces(place.sign_x)]
     for low in range(8):
         z = float(SPEED[15 - low])
         even = columns[0] + (z * z) * columns[2]
@@ -442,7 +443,7 @@
             at = step * 16 + v
             edge = recv[pl.ds(at, 8, stride=128), :]
             both = jnp.concatenate([edge, pltpu.roll(edge, HALF, 1)], axis=0)
-            both = jnp.where(mask, 0.0, both) * place.scale_x
+            both = jnp.where(mask, 0.0, both)
             inflow = jnp.concatenate([lift[p0] * both for p0 in range(4)], axis=0)
             hi, lo = split(right[at] + equilibrium + inflow)
             block = packed[at]
@@ -455,13 +456,14 @@
 
 
 def middle_kernel(
-    slabs, right_away, packed, recv, mixed, fresh_away, moments, planes, columns, sums, right, fresh, arrived, sent
+    slabs, right_away, packed, recv, mixed, fresh_away, moments_away, planes, columns, sums,
+    right, fresh, moments, arrived, sent, sent_moments,
 ):
     place = Place(slabs)
     mask = outgoing_mask(lane_index((16, 128)), place.sign_x)
     fetch, wait = stream([(lambda i: velocity_block(right_away, i), lambda i: velocity_block(right, i), arrived)])
     put, finish = stream([(lambda i: velocity_block(fresh, i), lambda i: velocity_block(fresh_away, i), sent)])
-    start_first(fetch)
+    start_all(fetch)
     split_planes(mixed, planes)
     sums[...] = jnp.zeros_like(sums)
 
@@ -470,7 +472,6 @@
             fresh[step * 16 + v] = column
 
         wait(step)
-        start_later(fetch, step)
         relax(place, step, right, packed, recv, planes, columns, mask, store)
         put(step)
         y = place.speed_y(step)
@@ -493,24 +494,29 @@
     lax.fori_loop(0, 8, loop, 0)
     for j in range(8):
         moments[pl.ds(j, 64, stride=8), :] = sums[j]
+    copy = pltpu.make_async_copy(moments, moments_away, sent_moments)
+    copy.start()
     for step in range(8):
         finish(step)
+    copy.wait()
 
 
 def middle(slabs, right, packed, recv, mixed):
     fresh, moments = pl.pallas_call(
         functools.partial(middle_kernel, slabs),
         in_specs=[HBM, VMEM, VMEM, VMEM],
-        out_specs=[HBM, VMEM],
-        out_shape=[pltpu.HBM((128, 64, 128), F32), kept(512, 128)],
+        out_specs=[HBM, HBM],
+        out_shape=[pltpu.HBM((128, 64, 128), F32), pltpu.HBM((512, 128), F32)],
         scratch_shapes=[
             pltpu.VMEM((8, 64, 128), F32),
             pltpu.VMEM((4, 64, 128), F32),
             pltpu.VMEM((8, 64, 128), F32),
             BLOCKS_V,
             BLOCKS_V,
+            pltpu.VMEM((512, 128), F32),
             SEMS,
             SEMS,
+            pltpu.SemaphoreType.DMA,
         ],
         compiler_params=PARAMS,
         name="middle",
@@ -523,7 +529,7 @@
     mask = outgoing_mask(lane_index((16, 128)), place.sign_x)
     fetch, wait = stream([(lambda i: velocity_block(right_away, i), lambda i: velocity_block(right, i), arrived)])
     put, finish = stream([(lambda i: blocks.at[i], lambda i: mode_block(out, i), sent)])
-    start_first(fetch)
+    start_all(fetch)
     split_planes(mixed, planes)
 
     def loop(step, carry):
@@ -533,7 +539,6 @@
             flat[pl.ds(v, 64, stride=16), :] = fresh
 
         wait(step)
-        start_later(fetch, step)
         relax(place, step, right, packed, recv, planes, columns, mask, store)
         put(step)
         return carry

time: 82.9 us -> 80.7 us (0.973)
  waiting for transfers between devices: 11.6 us -> 3.54 us
  starting transfers between devices: 26.2 us -> 33.8 us
  blocking collectives: 14.9 us -> 13.7 us
    all_to_all x3, starting transfers between devices: 20.2 us -> 28.9 us  [the longest x2 19.5 us: sum_over_velocities(): lax.all_to_all(partial_sums, 'vel', 0, 0, axis_index_groups=[ORDER])]
    all_to_all x3, waiting for transfers between devices: 11.6 us -> 3.54 us  [the longest x1 3.53 us: sum_over_velocities(): lax.all_to_all(mixed, 'vel', 0, 0, axis_index_groups=[ORDER])]
    all_to_all x1, blocking collectives: 14.9 us -> 13.7 us  [sum_over_velocities(): lax.all_to_all(mixed, 'vel', 0, 0, axis_index_groups=[ORDER])]
    ppermute x2, starting transfers between devices: 5.98 us -> 4.91 us  [body(): recv = lax.ppermute(send, axes, pairs).reshape(1024, 128)]
  transfers between devices with their start and end apart: 5 -> 5, of which waited for: 3 -> 1; matrix products, arithmetic and copies ran while one was open for 0% -> 0% of each run, Pallas kernels for 16% -> 17%
where the time goes in v3:
time: 80.7 us; the launch traced here: 80.3 us
  starting transfers between devices  33.8 us (42%)
  Pallas kernels  29.1 us (36%)
  blocking collectives  13.7 us (17%)
  waiting for transfers between devices  3.54 us (4%)
    all_to_all x2, starting transfers between devices, sum_over_velocities(): lax.all_to_all(partial_sums, 'vel', 0, 0, axis_index_groups=[ORDER])  19.5 us
    all_to_all x1, blocking collectives, sum_over_velocities(): lax.all_to_all(mixed, 'vel', 0, 0, axis_index_groups=[ORDER])  13.7 us
    all_to_all x1, starting transfers between devices, sum_over_velocities(): lax.all_to_all(mixed, 'vel', 0, 0, axis_index_groups=[ORDER])  9.35 us
    pallas_call x1, Pallas kernels, prepare_next(): pl.pallas_call(functools.partial(prepare_next_kernel, slabs), in_specs=[H...  5.78 us
    pallas_call x1, Pallas kernels, last(): pl.pallas_call(functools.partial(last_kernel, slabs), in_specs=[HBM, VMEM...  5.48 us
    pallas_call x1, Pallas kernels, middle(): pl.pallas_call(functools.partial(middle_kernel, slabs), in_specs=[HBM, VM...  5.41 us
    pallas_call x1, Pallas kernels, prepare(): pl.pallas_call(functools.partial(prepare_kernel, slabs), in_specs=[HBM],...  5.24 us
    ppermute x2, starting transfers between devices, body(): recv = lax.ppermute(send, axes, pairs).reshape(1024, 128)  4.91 us
  transfers between devices with their start and end apart: 5, of which 1 were waited for; matrix products, arithmetic and copies ran while one was open for 0% of the time, Pallas kernels for 17%

profile of v3, /device:TPU:1, one launch (start us, length us, event | category | flops | bytes accessed | tf_op | source)
XLA Modules:
  0.0 80.3 jit_solution(10740059914601201252)
XLA Ops:
  0.0 0.0 copy-start
  0.0 3.4 %first_moments.1 = f32[64,8,128]{2,1,0:T(8,128)} custom-call(f32[64,128,128]{2,1,0:T(8,128)} %bitcast.13), custom_call_target="tpu_custom_call" | custom-call | tf_op jit(solution)/shard_map/first_moments/pallas_call | solution.py:204
  3.4 11.7 %all-to-all-start = ((f32[32,16,128]{2,1,0:T(8,128)}), f32[32,16,128]{2,1,0:T(8,128)S(1)}, u32[]{:S(2)}, u32[]{:S(2)}) async-start(f32[32,16,128]{2,1,0:T(8,128)} %bitcast.17), calls=%async_computation | async-start | bytes 524288 | tf_op jit(solution)/shard_map/all_to_all | solution.py:267
  15.1 5.2 %prepare.1 = (f32[128,64,128]{2,1,0:T(8,128)}, f32[8,128,128]{2,1,0:T(8,128)}) custom-call(f32[64,128,128]{2,1,0:T(8,128)} %bitcast.14), custom_call_target="tpu_custom_call" | custom-call | tf_op jit(solution)/shard_map/prepare/pallas_call | solution.py:365
  20.3 0.0 all-to-all-done.gathered
  20.4 0.0 copy-done
  20.4 1.1 %mix_moments.2 = f32[32,16,128]{2,1,0:T(8,128)} custom-call(f32[256,256]{1,0:T(8,128)S(1)} %copy-done, f32[32,16,128]{2,1,0:T(8,128)S(1)} %all-to-all-done.gathered), custom_call_target="tpu_custom_call" | custom-call | tf_op jit(solution)/shard_map/mix_moments/pallas_call | solution.py:256
  21.4 3.0 %collective-permute-start = (f32[8,128,128]{2,1,0:T(8,128)}, f32[8,128,128]{2,1,0:T(8,128)S(1)}, u32[]{:S(2)}, u32[]{:S(2)}) collective-permute-start(f32[8,128,128]{2,1,0:T(8,128)} %get-tuple-element.29), channel_id=1, source_target_pairs={{16,48},{17,49},{18,50},{19,51},{20,52},{21,53},{22,54},{23,55},{2... | collective-permute-start | bytes 1572872 | tf_op jit(solution)/shard_map/ppermute | solution.py:587
  24.4 9.3 %all-to-all-start.1 = ((f32[32,16,128]{2,1,0:T(8,128)}), f32[32,16,128]{2,1,0:T(8,128)S(1)}, u32[]{:S(2)}, u32[]{:S(2)}) async-start(f32[32,16,128]{2,1,0:T(8,128)} %mix_moments.2), calls=%async_computation.1 | async-start | bytes 524288 | tf_op jit(solution)/shard_map/all_to_all | solution.py:271
  33.8 2.4 %pack.1.packed = bf16[128,64,128]{2,1,0:T(8,128)(2,1)S(1)} custom-call(f32[64,64,128]{2,1,0:T(8,128)} %bitcast.16), custom_call_target="tpu_custom_call" | custom-call | tf_op jit(solution)/shard_map/pack/pallas_call | solution.py:237
  36.2 3.5 %all-to-all-done.1 = f32[32,16,128]{2,1,0:T(8,128)S(1)} async-done(((f32[32,16,128]{2,1,0:T(8,128)}), f32[32,16,128]{2,1,0:T(8,128)S(1)}, u32[]{:S(2)}, u32[]{:S(2)}) %all-to-all-start.1) | async-done | bytes 262176 | tf_op jit(solution)/shard_map/all_to_all | solution.py:271
  39.7 0.0 collective-permute-done
  39.7 5.4 %middle.1 = (f32[128,64,128]{2,1,0:T(8,128)}, f32[512,128]{1,0:T(8,128)}) custom-call(f32[128,64,128]{2,1,0:T(8,128)} %get-tuple-element.28.right_away, bf16[128,64,128]{2,1,0:T(8,128)(2,1)S(1)} %pack.1.packed, f32[1024,128]{1,0:T(8,128)S(1)} %bitcast.11, f32[512,128]{1,0:T(8,128)S(1)} %bitcast.9), custom_call_target="tpu_custom_call" | custom-call | tf_op jit(solution)/shard_map/middle/pallas_call | solution.py:505
  45.2 7.8 %all-to-all-start.2 = ((f32[32,16,128]{2,1,0:T(8,128)}), f32[32,16,128]{2,1,0:T(8,128)S(1)}, u32[]{:S(2)}, u32[]{:S(2)}) async-start(f32[32,16,128]{2,1,0:T(8,128)} %bitcast.18), calls=%async_computation.2 | async-start | bytes 524288 | tf_op jit(solution)/shard_map/all_to_all | solution.py:267
  53.0 5.8 %prepare_next.1 = (f32[128,64,128]{2,1,0:T(8,128)}, f32[8,128,128]{2,1,0:T(8,128)S(1)}) custom-call(f32[128,64,128]{2,1,0:T(8,128)} %get-tuple-element.32.fresh, f32[64,128,128]{2,1,0:T(8,128)} %bitcast.15), custom_call_target="tpu_custom_call" | custom-call | tf_op jit(solution)/shard_map/prepare_next/pallas_call | solution.py:406
  58.8 0.0 all-to-all-done.2.gathered
  58.8 0.4 mix_moments.3
  59.2 1.9 %collective-permute-start.1 = (f32[8,128,128]{2,1,0:T(8,128)S(1)}, f32[8,128,128]{2,1,0:T(8,128)S(1)}, u32[]{:S(2)}, u32[]{:S(2)}) collective-permute-start(f32[8,128,128]{2,1,0:T(8,128)S(1)} %get-tuple-element.39), channel_id=1, source_target_pairs={{16,48},{17,49},{18,50},{19,51},{20,52},{21,53},{22,54},{23,55},{2... | collective-permute-start | bytes 1572872 | tf_op jit(solution)/shard_map/ppermute | solution.py:591
  61.1 13.7 %all_to_all.20 = f32[32,16,128]{2,1,0:T(8,128)S(1)} all-to-all(f32[32,16,128]{2,1,0:T(8,128)S(1)} %mix_moments.3), channel_id=1, replica_groups={{26,10,22,25,27,30,6,9,11,14,18,21,23,24,29,31,2,5,7,8,13,15,17,19,20,2..., dimensions={0} | all-to-all | bytes 524288 | tf_op jit(solution)/shard_map/all_to_all | solution.py:271
  74.8 0.0 collective-permute-done.1
  74.8 5.5 %last.1 = f32[64,128,128]{2,1,0:T(8,128)} custom-call(f32[128,64,128]{2,1,0:T(8,128)} %get-tuple-element.38.right_away, bf16[128,64,128]{2,1,0:T(8,128)(2,1)S(1)} %pack.1.packed, f32[1024,128]{1,0:T(8,128)S(1)} %bitcast.12, f32[512,128]{1,0:T(8,128)S(1)} %bitcast.10), custom_call_target="tpu_custom_call" | custom-call | tf_op jit(solution)/shard_map/last/pallas_call | solution.py:552
Async XLA Ops:
  0.0 20.4 %copy-start = (f32[256,256]{1,0:T(8,128)S(1)}, f32[256,256]{1,0:T(8,128)}, u32[]{:S(2)}) copy-start(f32[256,256]{1,0:T(8,128)} %constant.2.clone.mix) | copy-start | bytes 786436
  3.4 17.0 %all-to-all-start = ((f32[32,16,128]{2,1,0:T(8,128)}), f32[32,16,128]{2,1,0:T(8,128)S(1)}, u32[]{:S(2)}, u32[]{:S(2)}) async-start(f32[32,16,128]{2,1,0:T(8,128)} %bitcast.17), calls=%async_computation | async-start | bytes 524288 | tf_op jit(solution)/shard_map/all_to_all | solution.py:267
  21.4 18.3 %collective-permute-start = (f32[8,128,128]{2,1,0:T(8,128)}, f32[8,128,128]{2,1,0:T(8,128)S(1)}, u32[]{:S(2)}, u32[]{:S(2)}) collective-permute-start(f32[8,128,128]{2,1,0:T(8,128)} %get-tuple-element.29), channel_id=1, source_target_pairs={{16,48},{17,49},{18,50},{19,51},{20,52},{21,53},{22,54},{23,55},{2... | collective-permute-start | bytes 1572872 | tf_op jit(solution)/shard_map/ppermute | solution.py:587
  24.4 15.3 %all-to-all-start.1 = ((f32[32,16,128]{2,1,0:T(8,128)}), f32[32,16,128]{2,1,0:T(8,128)S(1)}, u32[]{:S(2)}, u32[]{:S(2)}) async-start(f32[32,16,128]{2,1,0:T(8,128)} %mix_moments.2), calls=%async_computation.1 | async-start | bytes 524288 | tf_op jit(solution)/shard_map/all_to_all | solution.py:271
  45.2 13.6 %all-to-all-start.2 = ((f32[32,16,128]{2,1,0:T(8,128)}), f32[32,16,128]{2,1,0:T(8,128)S(1)}, u32[]{:S(2)}, u32[]{:S(2)}) async-start(f32[32,16,128]{2,1,0:T(8,128)} %bitcast.18), calls=%async_computation.2 | async-start | bytes 524288 | tf_op jit(solution)/shard_map/all_to_all | solution.py:267
  59.2 15.6 %collective-permute-start.1 = (f32[8,128,128]{2,1,0:T(8,128)S(1)}, f32[8,128,128]{2,1,0:T(8,128)S(1)}, u32[]{:S(2)}, u32[]{:S(2)}) collective-permute-start(f32[8,128,128]{2,1,0:T(8,128)S(1)} %get-tuple-element.39), channel_id=1, source_target_pairs={{16,48},{17,49},{18,50},{19,51},{20,52},{21,53},{22,54},{23,55},{2... | collective-permute-start | bytes 1572872 | tf_op jit(solution)/shard_map/ppermute | solution.py:591

commit v4 on v3

--- a/solution.py
+++ b/solution.py
@@ -291,7 +291,6 @@
         scale_z = jnp.where(inside, speed, 0.0)
         wall_z = jnp.where(inside, 0.0, speed * (2.0 if up else lid))
         trace_z, lift_z = trace_face(1.0 if up else -1.0), lift_faces(1.0 if up else -1.0)
-        rows = pl.ds(pl.multiple_of(step * 16 + part * 8, 8), 8)
         face_x = [None] * 16
         for low in range(8):
             pair = []
@@ -300,7 +299,8 @@
                 turned = pltpu.roll(trace, HALF, 1)
                 pair.append((trace, turned))
                 face_x[r] = turned * scale_x
-            send[low, rows, :] = jnp.where(mask, pair[1][0], pair[0][1])
+            if send is not None:
+                send[part * 64 + low * 8 : part * 64 + low * 8 + 8, :] = jnp.where(mask, pair[1][0], pair[0][1])
         face_x[0] = face_x[0] + wall_x
         for p0 in range(4):
             x = [[source(part, p0 * 16 + p1 * 4 + p2) for p2 in range(4)] for p1 in range(4)]
@@ -340,7 +340,7 @@
     return read
 
 
-def prepare_kernel(slabs, prior, right, send, scratch, cells, made, arrived, sent):
+def prepare_kernel(slabs, prior, right, send, scratch, outgoing, cells, made, arrived, sent):
     place = Place(slabs)
     mask = outgoing_mask(lane_index((8, 128)), place.sign_x)
     fetch, wait = stream([(lambda i: mode_block(prior, i), lambda i: cells.at[i], arrived)])
@@ -350,9 +350,10 @@
     def loop(step, carry):
         wait(step)
         read = block_reader(cells.at[step])
-        add_inflow(read, read, scratch, send, place, step, mask)
+        add_inflow(read, read, scratch, outgoing, place, step, mask)
         for v in range(16):
             made[step * 16 + v] = scratch[velocity_rows(v), :]
+            send[step * 16 + v] = outgoing[pl.ds(v // 8 * 64 + v % 8, 8, stride=8), :]
         put(step)
         return carry
 
@@ -366,15 +367,15 @@
         functools.partial(prepare_kernel, slabs),
         in_specs=[HBM],
         out_specs=[HBM, VMEM],
-        out_shape=[pltpu.HBM((128, 64, 128), F32), kept(8, 128, 128)],
-        scratch_shapes=[pltpu.VMEM((1024, 128), F32), BLOCKS_Q, BLOCKS_V, SEMS, SEMS],
+        out_shape=[pltpu.HBM((128, 64, 128), F32), kept(128, 8, 128)],
+        scratch_shapes=[pltpu.VMEM((1024, 128), F32), pltpu.VMEM((128, 128), F32), BLOCKS_Q, BLOCKS_V, SEMS, SEMS],
         compiler_params=PARAMS,
         name="prepare",
     )(away(prior))
 
 
 def prepare_next_kernel(
-    slabs, fresh, prior, right, send, rows, scratch, columns, cells, made, arrived, arrived_prior, sent
+    slabs, fresh, prior, right, rows, scratch, columns, cells, made, arrived, arrived_prior, sent
 ):
     place = Place(slabs)
     mask = outgoing_mask(lane_index((8, 128)), place.sign_x)
@@ -391,7 +392,7 @@
         wait(step)
         for v in range(16):
             rows[velocity_rows(v), :] = columns[step * 16 + v]
-        add_inflow(row_reader(rows), block_reader(cells.at[step]), scratch, send, place, step, mask)
+        add_inflow(row_reader(rows), block_reader(cells.at[step]), scratch, None, place, step, mask)
         for v in range(16):
             made[step * 16 + v] = scratch[velocity_rows(v), :]
         put(step)
@@ -406,8 +407,8 @@
     return pl.pallas_call(
         functools.partial(prepare_next_kernel, slabs),
         in_specs=[HBM, HBM],
-        out_specs=[HBM, VMEM],
-        out_shape=[pltpu.HBM((128, 64, 128), F32), kept(8, 128, 128)],
+        out_specs=HBM,
+        out_shape=pltpu.HBM((128, 64, 128), F32),
         scratch_shapes=[
             pltpu.VMEM((1024, 128), F32),
             pltpu.VMEM((1024, 128), F32),
@@ -441,7 +442,7 @@
         odd = z * columns[1] + (z * z * z) * columns[3]
         for v, equilibrium in ((low, even - odd), (15 - low, even + odd)):
             at = step * 16 + v
-            edge = recv[pl.ds(at, 8, stride=128), :]
+            edge = recv[at]
             both = jnp.concatenate([edge, pltpu.roll(edge, HALF, 1)], axis=0)
             both = jnp.where(mask, 0.0, both)
             inflow = jnp.concatenate([lift[p0] * both for p0 in range(4)], axis=0)
@@ -456,13 +457,19 @@
 
 
 def middle_kernel(
-    slabs, right_away, packed, recv, mixed, fresh_away, moments_away, planes, columns, sums,
-    right, fresh, moments, arrived, sent, sent_moments,
+    slabs, right_away, packed, recv, mixed, fresh_away, moments_away, send_away, planes, columns, sums,
+    right, fresh, moments, send, arrived, sent, sent_moments, sent_send,
 ):
     place = Place(slabs)
     mask = outgoing_mask(lane_index((16, 128)), place.sign_x)
+    face = trace_face(place.sign_x)
     fetch, wait = stream([(lambda i: velocity_block(right_away, i), lambda i: velocity_block(right, i), arrived)])
-    put, finish = stream([(lambda i: velocity_block(fresh, i), lambda i: velocity_block(fresh_away, i), sent)])
+    put, finish = stream(
+        [
+            (lambda i: velocity_block(fresh, i), lambda i: velocity_block(fresh_away, i), sent),
+            (lambda i: velocity_block(send, i), lambda i: velocity_block(send_away, i), sent_send),
+        ]
+    )
     start_all(fetch)
     split_planes(mixed, planes)
     sums[...] = jnp.zeros_like(sums)
@@ -470,6 +477,9 @@
     def loop(step, carry):
         def store(v, column):
             fresh[step * 16 + v] = column
+            trace = sum(face[p0] * column[p0 * 16 : p0 * 16 + 16] for p0 in range(4))
+            outgoing = jnp.where(mask[:8], trace[8:], pltpu.roll(trace[:8], HALF, 1))
+            send[step * 16 + v] = outgoing
 
         wait(step)
         relax(place, step, right, packed, recv, planes, columns, mask, store)
@@ -502,11 +512,11 @@
 
 
 def middle(slabs, right, packed, recv, mixed):
-    fresh, moments = pl.pallas_call(
+    fresh, moments, send = pl.pallas_call(
         functools.partial(middle_kernel, slabs),
         in_specs=[HBM, VMEM, VMEM, VMEM],
-        out_specs=[HBM, HBM],
-        out_shape=[pltpu.HBM((128, 64, 128), F32), pltpu.HBM((512, 128), F32)],
+        out_specs=[HBM] * 3,
+        out_shape=[pltpu.HBM((128, 64, 128), F32), pltpu.HBM((512, 128), F32), pltpu.HBM((128, 8, 128), F32)],
         scratch_shapes=[
             pltpu.VMEM((8, 64, 128), F32),
             pltpu.VMEM((4, 64, 128), F32),
@@ -514,14 +524,16 @@
             BLOCKS_V,
             BLOCKS_V,
             pltpu.VMEM((512, 128), F32),
+            pltpu.VMEM((128, 8, 128), F32),
             SEMS,
             SEMS,
             pltpu.SemaphoreType.DMA,
+            SEMS,
         ],
         compiler_params=PARAMS,
         name="middle",
     )(away(right), here(packed), here(recv), here(mixed))
-    return fresh, moments.reshape(VEL, 16, 128)
+    return fresh, moments.reshape(VEL, 16, 128), send
 
 
 def last_kernel(slabs, right_away, packed, recv, mixed, out, planes, columns, right, blocks, arrived, sent):
@@ -584,11 +596,11 @@
     cells = prior.reshape(64, 128, 128)
     moments = first_moments(cells)
     mixed, (right, send) = sum_over_velocities(mix, moments, prepare(slabs, cells))
-    recv = lax.ppermute(send, axes, pairs).reshape(1024, 128)
+    recv = lax.ppermute(send, axes, pairs)
     packed = pack(block_inverse)
-    fresh, moments = middle(slabs, right, packed, recv, mixed)
-    mixed, (right, send) = sum_over_velocities(mix, moments, prepare_next(slabs, fresh, cells))
-    recv = lax.ppermute(send, axes, pairs).reshape(1024, 128)
+    fresh, moments, send = middle(slabs, right, packed, recv, mixed)
+    recv = lax.ppermute(send, axes, pairs)
+    mixed, right = sum_over_velocities(mix, moments, prepare_next(slabs, fresh, cells))
     return last(slabs, right, packed, recv, mixed).reshape(prior.shape)
 
 

time: 80.7 us -> 79.1 us (0.980)
  blocking collectives: 13.7 us -> 10.8 us
    all_to_all x1, blocking collectives: 13.7 us -> 10.8 us  [sum_over_velocities(): lax.all_to_all(mixed, 'vel', 0, 0, axis_index_groups=[ORDER])]
  transfers between devices with their start and end apart: 5 -> 5, of which waited for: 1 -> 2; matrix products, arithmetic and copies ran while one was open for 0% -> 0% of each run, Pallas kernels for 17% -> 18%
where the time goes in v4:
time: 79.1 us; the launch traced here: 78.7 us
  starting transfers between devices  34.4 us (43%)
  Pallas kernels  29.7 us (38%)
  blocking collectives  10.8 us (14%)
  waiting for transfers between devices  3.67 us (5%)
    all_to_all x2, starting transfers between devices, sum_over_velocities(): lax.all_to_all(partial_sums, 'vel', 0, 0, axis_index_groups=[ORDER])  20.2 us
    all_to_all x1, blocking collectives, sum_over_velocities(): lax.all_to_all(mixed, 'vel', 0, 0, axis_index_groups=[ORDER])  10.8 us
    all_to_all x1, starting transfers between devices, sum_over_velocities(): lax.all_to_all(mixed, 'vel', 0, 0, axis_index_groups=[ORDER])  9.28 us
    pallas_call x1, Pallas kernels, middle(): pl.pallas_call(functools.partial(middle_kernel, slabs), in_specs=[HBM, VM...  5.87 us
    pallas_call x1, Pallas kernels, prepare_next(): pl.pallas_call(functools.partial(prepare_next_kernel, slabs), in_specs=[H...  5.8 us
    pallas_call x1, Pallas kernels, last(): pl.pallas_call(functools.partial(last_kernel, slabs), in_specs=[HBM, VMEM...  5.48 us
    pallas_call x1, Pallas kernels, prepare(): pl.pallas_call(functools.partial(prepare_kernel, slabs), in_specs=[HBM],...  5.31 us
    ppermute x2, starting transfers between devices, body(): recv = lax.ppermute(send, axes, pairs)  4.91 us
  transfers between devices with their start and end apart: 5, of which 2 were waited for; matrix products, arithmetic and copies ran while one was open for 0% of the time, Pallas kernels for 18%

profile of v4, /device:TPU:1, one launch (start us, length us, event | category | flops | bytes accessed | tf_op | source)
XLA Modules:
  0.0 78.7 jit_solution(2131895109356750639)
XLA Ops:
  0.0 0.0 copy-start
  0.0 3.4 %first_moments.1 = f32[64,8,128]{2,1,0:T(8,128)} custom-call(f32[64,128,128]{2,1,0:T(8,128)} %bitcast.9), custom_call_target="tpu_custom_call" | custom-call | tf_op jit(solution)/shard_map/first_moments/pallas_call | solution.py:204
  3.4 11.7 %all-to-all-start = ((f32[32,16,128]{2,1,0:T(8,128)}), f32[32,16,128]{2,1,0:T(8,128)S(1)}, u32[]{:S(2)}, u32[]{:S(2)}) async-start(f32[32,16,128]{2,1,0:T(8,128)} %bitcast.13), calls=%async_computation | async-start | bytes 524288 | tf_op jit(solution)/shard_map/all_to_all | solution.py:267
  15.1 5.3 %prepare.1 = (f32[128,64,128]{2,1,0:T(8,128)}, f32[128,8,128]{2,1,0:T(8,128)}) custom-call(f32[64,128,128]{2,1,0:T(8,128)} %bitcast.10), custom_call_target="tpu_custom_call" | custom-call | tf_op jit(solution)/shard_map/prepare/pallas_call | solution.py:366
  20.4 0.0 all-to-all-done.gathered
  20.4 0.0 copy-done
  20.4 1.1 %mix_moments.2 = f32[32,16,128]{2,1,0:T(8,128)} custom-call(f32[256,256]{1,0:T(8,128)S(1)} %copy-done, f32[32,16,128]{2,1,0:T(8,128)S(1)} %all-to-all-done.gathered), custom_call_target="tpu_custom_call" | custom-call | tf_op jit(solution)/shard_map/mix_moments/pallas_call | solution.py:256
  21.5 3.0 %collective-permute-start = (f32[128,8,128]{2,1,0:T(8,128)}, f32[128,8,128]{2,1,0:T(8,128)S(1)}, u32[]{:S(2)}, u32[]{:S(2)}) collective-permute-start(f32[128,8,128]{2,1,0:T(8,128)} %get-tuple-element.26), channel_id=1, source_target_pairs={{16,48},{17,49},{18,50},{19,51},{20,52},{21,53},{22,54},{23,55},{2... | collective-permute-start | bytes 1572872 | tf_op jit(solution)/shard_map/ppermute | solution.py:599
  24.5 9.3 %all-to-all-start.1 = ((f32[32,16,128]{2,1,0:T(8,128)}), f32[32,16,128]{2,1,0:T(8,128)S(1)}, u32[]{:S(2)}, u32[]{:S(2)}) async-start(f32[32,16,128]{2,1,0:T(8,128)} %mix_moments.2), calls=%async_computation.1 | async-start | bytes 524288 | tf_op jit(solution)/shard_map/all_to_all | solution.py:271
  33.8 2.4 %pack.1.packed = bf16[128,64,128]{2,1,0:T(8,128)(2,1)S(1)} custom-call(f32[64,64,128]{2,1,0:T(8,128)} %bitcast.12), custom_call_target="tpu_custom_call" | custom-call | tf_op jit(solution)/shard_map/pack/pallas_call | solution.py:237
  36.2 3.5 %all-to-all-done.1 = f32[32,16,128]{2,1,0:T(8,128)S(1)} async-done(((f32[32,16,128]{2,1,0:T(8,128)}), f32[32,16,128]{2,1,0:T(8,128)S(1)}, u32[]{:S(2)}, u32[]{:S(2)}) %all-to-all-start.1) | async-done | bytes 262176 | tf_op jit(solution)/shard_map/all_to_all | solution.py:271
  39.7 0.0 collective-permute-done.recv
  39.8 5.9 %middle.1 = (f32[128,64,128]{2,1,0:T(8,128)}, f32[512,128]{1,0:T(8,128)}, f32[128,8,128]{2,1,0:T(8,128)}) custom-call(f32[128,64,128]{2,1,0:T(8,128)} %get-tuple-element.25.right_away, bf16[128,64,128]{2,1,0:T(8,128)(2,1)S(1)} %pack.1.packed, f32[128,8,128]{2,1,0:T(8,128)S(1)} %collective-permute-done.recv, f32[512,128]{1,0:T(8,128)S(1)} %bitcast.7), custom_call_target="tpu_custom_call" | custom-call | tf_op jit(solution)/shard_map/middle/pallas_call | solution.py:515
  45.6 1.9 %collective-permute-start.1 = (f32[128,8,128]{2,1,0:T(8,128)}, f32[128,8,128]{2,1,0:T(8,128)S(1)}, u32[]{:S(2)}, u32[]{:S(2)}) collective-permute-start(f32[128,8,128]{2,1,0:T(8,128)} %get-tuple-element.33), channel_id=1, source_target_pairs={{16,48},{17,49},{18,50},{19,51},{20,52},{21,53},{22,54},{23,55},{2... | collective-permute-start | bytes 1572872 | tf_op jit(solution)/shard_map/ppermute | solution.py:602
  47.6 8.4 %all-to-all-start.2 = ((f32[32,16,128]{2,1,0:T(8,128)}), f32[32,16,128]{2,1,0:T(8,128)S(1)}, u32[]{:S(2)}, u32[]{:S(2)}) async-start(f32[32,16,128]{2,1,0:T(8,128)} %bitcast.14), calls=%async_computation.2 | async-start | bytes 524288 | tf_op jit(solution)/shard_map/all_to_all | solution.py:267
  56.0 5.8 %prepare_next.1.right_away = f32[128,64,128]{2,1,0:T(8,128)} custom-call(f32[128,64,128]{2,1,0:T(8,128)} %get-tuple-element.29.fresh, f32[64,128,128]{2,1,0:T(8,128)} %bitcast.11), custom_call_target="tpu_custom_call" | custom-call | tf_op jit(solution)/shard_map/prepare_next/pallas_call | solution.py:407
  61.8 0.1 all-to-all-done.2.gathered
  62.0 0.4 mix_moments.3
  62.3 10.8 %all_to_all.20 = f32[32,16,128]{2,1,0:T(8,128)S(1)} all-to-all(f32[32,16,128]{2,1,0:T(8,128)S(1)} %mix_moments.3), channel_id=1, replica_groups={{26,10,22,25,27,30,6,9,11,14,18,21,23,24,29,31,2,5,7,8,13,15,17,19,20,2..., dimensions={0} | all-to-all | bytes 524288 | tf_op jit(solution)/shard_map/all_to_all | solution.py:271
  73.2 0.0 collective-permute-done.1.recv
  73.2 5.5 %last.1 = f32[64,128,128]{2,1,0:T(8,128)} custom-call(f32[128,64,128]{2,1,0:T(8,128)} %prepare_next.1.right_away, bf16[128,64,128]{2,1,0:T(8,128)(2,1)S(1)} %pack.1.packed, f32[128,8,128]{2,1,0:T(8,128)S(1)} %collective-permute-done.1.recv, f32[512,128]{1,0:T(8,128)S(1)} %bitcast.8), custom_call_target="tpu_custom_call" | custom-call | tf_op jit(solution)/shard_map/last/pallas_call | solution.py:564
Async XLA Ops:
  0.0 20.4 %copy-start = (f32[256,256]{1,0:T(8,128)S(1)}, f32[256,256]{1,0:T(8,128)}, u32[]{:S(2)}) copy-start(f32[256,256]{1,0:T(8,128)} %constant.2.clone.mix) | copy-start | bytes 786436
  3.4 17.0 %all-to-all-start = ((f32[32,16,128]{2,1,0:T(8,128)}), f32[32,16,128]{2,1,0:T(8,128)S(1)}, u32[]{:S(2)}, u32[]{:S(2)}) async-start(f32[32,16,128]{2,1,0:T(8,128)} %bitcast.13), calls=%async_computation | async-start | bytes 524288 | tf_op jit(solution)/shard_map/all_to_all | solution.py:267
  21.5 18.2 %collective-permute-start = (f32[128,8,128]{2,1,0:T(8,128)}, f32[128,8,128]{2,1,0:T(8,128)S(1)}, u32[]{:S(2)}, u32[]{:S(2)}) collective-permute-start(f32[128,8,128]{2,1,0:T(8,128)} %get-tuple-element.26), channel_id=1, source_target_pairs={{16,48},{17,49},{18,50},{19,51},{20,52},{21,53},{22,54},{23,55},{2... | collective-permute-start | bytes 1572872 | tf_op jit(solution)/shard_map/ppermute | solution.py:599
  24.5 15.2 %all-to-all-start.1 = ((f32[32,16,128]{2,1,0:T(8,128)}), f32[32,16,128]{2,1,0:T(8,128)S(1)}, u32[]{:S(2)}, u32[]{:S(2)}) async-start(f32[32,16,128]{2,1,0:T(8,128)} %mix_moments.2), calls=%async_computation.1 | async-start | bytes 524288 | tf_op jit(solution)/shard_map/all_to_all | solution.py:271
  45.6 27.5 %collective-permute-start.1 = (f32[128,8,128]{2,1,0:T(8,128)}, f32[128,8,128]{2,1,0:T(8,128)S(1)}, u32[]{:S(2)}, u32[]{:S(2)}) collective-permute-start(f32[128,8,128]{2,1,0:T(8,128)} %get-tuple-element.33), channel_id=1, source_target_pairs={{16,48},{17,49},{18,50},{19,51},{20,52},{21,53},{22,54},{23,55},{2... | collective-permute-start | bytes 1572872 | tf_op jit(solution)/shard_map/ppermute | solution.py:602
  47.6 14.4 %all-to-all-start.2 = ((f32[32,16,128]{2,1,0:T(8,128)}), f32[32,16,128]{2,1,0:T(8,128)S(1)}, u32[]{:S(2)}, u32[]{:S(2)}) async-start(f32[32,16,128]{2,1,0:T(8,128)} %bitcast.14), calls=%async_computation.2 | async-start | bytes 524288 | tf_op jit(solution)/shard_map/all_to_all | solution.py:267

commit v5 on v4

--- a/solution.py
+++ b/solution.py
@@ -23,11 +23,11 @@
 
 
 def ring_hops(vel):
-    y, z = vel // 4 % 4, vel % 4
-    return vel // 16 + min(y, 4 - y) + min(z, 4 - z)
-
-
-ORDER = sorted(range(VEL), key=lambda vel: -ring_hops(vel))
+    along_y, along_z = min(vel // 4 % 4, 4 - vel // 4 % 4), min(vel % 4, 4 - vel % 4)
+    return vel // 16, along_y + along_z, vel
+
+
+ORDER = sorted(range(VEL), key=ring_hops, reverse=True)
 
 
 def grid_speed(index):

time: 79.1 us -> 78.4 us (level)
  transfers between devices with their start and end apart: 5 -> 5, of which waited for: 2 -> 1; matrix products, arithmetic and copies ran while one was open for 0% -> 0% of each run, Pallas kernels for 18% -> 18%
where the time goes in v5:
time: 78.4 us; the launch traced here: 77.9 us
  starting transfers between devices  34 us (43%)
  Pallas kernels  29.7 us (38%)
  blocking collectives  10.9 us (14%)
  waiting for transfers between devices  3.18 us (4%)
    all_to_all x2, starting transfers between devices, sum_over_velocities(): lax.all_to_all(partial_sums, 'vel', 0, 0, axis_index_groups=[ORDER])  20.3 us
    all_to_all x1, blocking collectives, sum_over_velocities(): lax.all_to_all(mixed, 'vel', 0, 0, axis_index_groups=[ORDER])  10.9 us
    all_to_all x1, starting transfers between devices, sum_over_velocities(): lax.all_to_all(mixed, 'vel', 0, 0, axis_index_groups=[ORDER])  8.85 us
    pallas_call x1, Pallas kernels, middle(): pl.pallas_call(functools.partial(middle_kernel, slabs), in_specs=[HBM, VM...  5.88 us
    pallas_call x1, Pallas kernels, prepare_next(): pl.pallas_call(functools.partial(prepare_next_kernel, slabs), in_specs=[H...  5.8 us
    pallas_call x1, Pallas kernels, last(): pl.pallas_call(functools.partial(last_kernel, slabs), in_specs=[HBM, VMEM...  5.48 us
    pallas_call x1, Pallas kernels, prepare(): pl.pallas_call(functools.partial(prepare_kernel, slabs), in_specs=[HBM],...  5.31 us
    ppermute x2, starting transfers between devices, body(): recv = lax.ppermute(send, axes, pairs)  4.91 us
  transfers between devices with their start and end apart: 5, of which 1 were waited for; matrix products, arithmetic and copies ran while one was open for 0% of the time, Pallas kernels for 18%

profile of v5, /device:TPU:1, one launch (start us, length us, event | category | flops | bytes accessed | tf_op | source)
XLA Modules:
  0.0 77.9 jit_solution(4252365479582587384)
XLA Ops:
  0.0 0.0 copy-start
  0.0 3.4 %first_moments.1 = f32[64,8,128]{2,1,0:T(8,128)} custom-call(f32[64,128,128]{2,1,0:T(8,128)} %bitcast.9), custom_call_target="tpu_custom_call" | custom-call | tf_op jit(solution)/shard_map/first_moments/pallas_call | solution.py:204
  3.4 11.7 %all-to-all-start = ((f32[32,16,128]{2,1,0:T(8,128)}), f32[32,16,128]{2,1,0:T(8,128)S(1)}, u32[]{:S(2)}, u32[]{:S(2)}) async-start(f32[32,16,128]{2,1,0:T(8,128)} %bitcast.13), calls=%async_computation | async-start | bytes 524288 | tf_op jit(solution)/shard_map/all_to_all | solution.py:267
  15.1 5.3 %prepare.1 = (f32[128,64,128]{2,1,0:T(8,128)}, f32[128,8,128]{2,1,0:T(8,128)}) custom-call(f32[64,128,128]{2,1,0:T(8,128)} %bitcast.10), custom_call_target="tpu_custom_call" | custom-call | tf_op jit(solution)/shard_map/prepare/pallas_call | solution.py:366
  20.4 0.0 all-to-all-done.gathered
  20.4 0.0 copy-done
  20.4 1.1 %mix_moments.2 = f32[32,16,128]{2,1,0:T(8,128)} custom-call(f32[256,256]{1,0:T(8,128)S(1)} %copy-done, f32[32,16,128]{2,1,0:T(8,128)S(1)} %all-to-all-done.gathered), custom_call_target="tpu_custom_call" | custom-call | tf_op jit(solution)/shard_map/mix_moments/pallas_call | solution.py:256
  21.5 3.0 %collective-permute-start = (f32[128,8,128]{2,1,0:T(8,128)}, f32[128,8,128]{2,1,0:T(8,128)S(1)}, u32[]{:S(2)}, u32[]{:S(2)}) collective-permute-start(f32[128,8,128]{2,1,0:T(8,128)} %get-tuple-element.26), channel_id=1, source_target_pairs={{16,48},{17,49},{18,50},{19,51},{20,52},{21,53},{22,54},{23,55},{2... | collective-permute-start | bytes 1572872 | tf_op jit(solution)/shard_map/ppermute | solution.py:599
  24.5 8.8 %all-to-all-start.1 = ((f32[32,16,128]{2,1,0:T(8,128)}), f32[32,16,128]{2,1,0:T(8,128)S(1)}, u32[]{:S(2)}, u32[]{:S(2)}) async-start(f32[32,16,128]{2,1,0:T(8,128)} %mix_moments.2), calls=%async_computation.1 | async-start | bytes 524288 | tf_op jit(solution)/shard_map/all_to_all | solution.py:271
  33.4 2.4 %pack.1.packed = bf16[128,64,128]{2,1,0:T(8,128)(2,1)S(1)} custom-call(f32[64,64,128]{2,1,0:T(8,128)} %bitcast.12), custom_call_target="tpu_custom_call" | custom-call | tf_op jit(solution)/shard_map/pack/pallas_call | solution.py:237
  35.8 3.2 %all-to-all-done.1 = f32[32,16,128]{2,1,0:T(8,128)S(1)} async-done(((f32[32,16,128]{2,1,0:T(8,128)}), f32[32,16,128]{2,1,0:T(8,128)S(1)}, u32[]{:S(2)}, u32[]{:S(2)}) %all-to-all-start.1) | async-done | bytes 262176 | tf_op jit(solution)/shard_map/all_to_all | solution.py:271
  39.0 0.0 collective-permute-done.recv
  39.0 5.9 %middle.1 = (f32[128,64,128]{2,1,0:T(8,128)}, f32[512,128]{1,0:T(8,128)}, f32[128,8,128]{2,1,0:T(8,128)}) custom-call(f32[128,64,128]{2,1,0:T(8,128)} %get-tuple-element.25.right_away, bf16[128,64,128]{2,1,0:T(8,128)(2,1)S(1)} %pack.1.packed, f32[128,8,128]{2,1,0:T(8,128)S(1)} %collective-permute-done.recv, f32[512,128]{1,0:T(8,128)S(1)} %bitcast.7), custom_call_target="tpu_custom_call" | custom-call | tf_op jit(solution)/shard_map/middle/pallas_call | solution.py:515
  44.8 1.9 %collective-permute-start.1 = (f32[128,8,128]{2,1,0:T(8,128)}, f32[128,8,128]{2,1,0:T(8,128)S(1)}, u32[]{:S(2)}, u32[]{:S(2)}) collective-permute-start(f32[128,8,128]{2,1,0:T(8,128)} %get-tuple-element.33), channel_id=1, source_target_pairs={{16,48},{17,49},{18,50},{19,51},{20,52},{21,53},{22,54},{23,55},{2... | collective-permute-start | bytes 1572872 | tf_op jit(solution)/shard_map/ppermute | solution.py:602
  46.8 8.5 %all-to-all-start.2 = ((f32[32,16,128]{2,1,0:T(8,128)}), f32[32,16,128]{2,1,0:T(8,128)S(1)}, u32[]{:S(2)}, u32[]{:S(2)}) async-start(f32[32,16,128]{2,1,0:T(8,128)} %bitcast.14), calls=%async_computation.2 | async-start | bytes 524288 | tf_op jit(solution)/shard_map/all_to_all | solution.py:267
  55.3 5.8 %prepare_next.1.right_away = f32[128,64,128]{2,1,0:T(8,128)} custom-call(f32[128,64,128]{2,1,0:T(8,128)} %get-tuple-element.29.fresh, f32[64,128,128]{2,1,0:T(8,128)} %bitcast.11), custom_call_target="tpu_custom_call" | custom-call | tf_op jit(solution)/shard_map/prepare_next/pallas_call | solution.py:407
  61.1 0.0 all-to-all-done.2.gathered
  61.1 0.4 mix_moments.3
  61.5 10.9 %all_to_all.20 = f32[32,16,128]{2,1,0:T(8,128)S(1)} all-to-all(f32[32,16,128]{2,1,0:T(8,128)S(1)} %mix_moments.3), channel_id=1, replica_groups={{26,30,27,25,22,31,29,24,23,21,18,28,20,19,17,16,10,14,11,9,6,15,13,8,7..., dimensions={0} | all-to-all | bytes 524288 | tf_op jit(solution)/shard_map/all_to_all | solution.py:271
  72.4 0.0 collective-permute-done.1.recv
  72.4 5.5 %last.1 = f32[64,128,128]{2,1,0:T(8,128)} custom-call(f32[128,64,128]{2,1,0:T(8,128)} %prepare_next.1.right_away, bf16[128,64,128]{2,1,0:T(8,128)(2,1)S(1)} %pack.1.packed, f32[128,8,128]{2,1,0:T(8,128)S(1)} %collective-permute-done.1.recv, f32[512,128]{1,0:T(8,128)S(1)} %bitcast.8), custom_call_target="tpu_custom_call" | custom-call | tf_op jit(solution)/shard_map/last/pallas_call | solution.py:564
Async XLA Ops:
  0.0 20.4 %copy-start = (f32[256,256]{1,0:T(8,128)S(1)}, f32[256,256]{1,0:T(8,128)}, u32[]{:S(2)}) copy-start(f32[256,256]{1,0:T(8,128)} %constant.2.clone.mix) | copy-start | bytes 786436
  3.4 17.0 %all-to-all-start = ((f32[32,16,128]{2,1,0:T(8,128)}), f32[32,16,128]{2,1,0:T(8,128)S(1)}, u32[]{:S(2)}, u32[]{:S(2)}) async-start(f32[32,16,128]{2,1,0:T(8,128)} %bitcast.13), calls=%async_computation | async-start | bytes 524288 | tf_op jit(solution)/shard_map/all_to_all | solution.py:267
  21.5 17.4 %collective-permute-start = (f32[128,8,128]{2,1,0:T(8,128)}, f32[128,8,128]{2,1,0:T(8,128)S(1)}, u32[]{:S(2)}, u32[]{:S(2)}) collective-permute-start(f32[128,8,128]{2,1,0:T(8,128)} %get-tuple-element.26), channel_id=1, source_target_pairs={{16,48},{17,49},{18,50},{19,51},{20,52},{21,53},{22,54},{23,55},{2... | collective-permute-start | bytes 1572872 | tf_op jit(solution)/shard_map/ppermute | solution.py:599
  24.5 14.4 %all-to-all-start.1 = ((f32[32,16,128]{2,1,0:T(8,128)}), f32[32,16,128]{2,1,0:T(8,128)S(1)}, u32[]{:S(2)}, u32[]{:S(2)}) async-start(f32[32,16,128]{2,1,0:T(8,128)} %mix_moments.2), calls=%async_computation.1 | async-start | bytes 524288 | tf_op jit(solution)/shard_map/all_to_all | solution.py:271
  44.8 27.6 %collective-permute-start.1 = (f32[128,8,128]{2,1,0:T(8,128)}, f32[128,8,128]{2,1,0:T(8,128)S(1)}, u32[]{:S(2)}, u32[]{:S(2)}) collective-permute-start(f32[128,8,128]{2,1,0:T(8,128)} %get-tuple-element.33), channel_id=1, source_target_pairs={{16,48},{17,49},{18,50},{19,51},{20,52},{21,53},{22,54},{23,55},{2... | collective-permute-start | bytes 1572872 | tf_op jit(solution)/shard_map/ppermute | solution.py:602
  46.8 14.4 %all-to-all-start.2 = ((f32[32,16,128]{2,1,0:T(8,128)}), f32[32,16,128]{2,1,0:T(8,128)S(1)}, u32[]{:S(2)}, u32[]{:S(2)}) async-start(f32[32,16,128]{2,1,0:T(8,128)} %bitcast.14), calls=%async_computation.2 | async-start | bytes 524288 | tf_op jit(solution)/shard_map/all_to_all | solution.py:267

commit v6 on v5

--- a/solution.py
+++ b/solution.py
@@ -181,22 +181,27 @@
     return jnp.concatenate([half, half], axis=1)
 
 
+FIRST = 16
+FIRST_SEMS = pltpu.SemaphoreType.DMA((64 // FIRST,))
+
+
 def first_moments_kernel(prior, moments, cells, sums, arrived, sent):
     def part(ref, step):
-        return ref.at[pl.ds(step * 8, 8)]
+        return ref.at[pl.ds(step * FIRST, FIRST)]
 
     fetch, wait = stream([(lambda i: part(prior, i), lambda i: part(cells, i), arrived)])
     put, finish = stream([(lambda i: part(sums, i), lambda i: part(moments, i), sent)])
-    start_all(fetch)
+    for step in range(64 // FIRST):
+        fetch(step)
     weights = moment_weights(lax.axis_index("vel") % 2 * LOCAL_Y)
-    for step in range(8):
+    for step in range(64 // FIRST):
         wait(step)
-        for q in range(step * 8, step * 8 + 8):
+        for q in range(step * FIRST, step * FIRST + FIRST):
             hi, lo = split(cells[q])
             product = jnp.dot(weights, jnp.concatenate([hi, lo], axis=0), preferred_element_type=F32)
             sums[q] = product[:8] + product[8:]
         put(step)
-    for step in range(8):
+    for step in range(64 // FIRST):
         finish(step)
 
 
@@ -206,7 +211,7 @@
         in_specs=[HBM],
         out_specs=HBM,
         out_shape=pltpu.HBM((64, 8, 128), F32),
-        scratch_shapes=[pltpu.VMEM((64, 128, 128), F32), pltpu.VMEM((64, 8, 128), F32), SEMS, SEMS],
+        scratch_shapes=[pltpu.VMEM((64, 128, 128), F32), pltpu.VMEM((64, 8, 128), F32), FIRST_SEMS, FIRST_SEMS],
         compiler_params=PARAMS,
         name="first_moments",
     )(away(prior)).reshape(VEL, 16, 128)
@@ -340,11 +345,18 @@
     return read
 
 
-def prepare_kernel(slabs, prior, right, send, scratch, outgoing, cells, made, arrived, sent):
+def prepare_kernel(
+    slabs, prior, right, send_away, scratch, outgoing, cells, made, send, arrived, sent, sent_send
+):
     place = Place(slabs)
     mask = outgoing_mask(lane_index((8, 128)), place.sign_x)
     fetch, wait = stream([(lambda i: mode_block(prior, i), lambda i: cells.at[i], arrived)])
-    put, finish = stream([(lambda i: velocity_block(made, i), lambda i: velocity_block(right, i), sent)])
+    put, finish = stream(
+        [
+            (lambda i: velocity_block(made, i), lambda i: velocity_block(right, i), sent),
+            (lambda i: velocity_block(send, i), lambda i: velocity_block(send_away, i), sent_send),
+        ]
+    )
     start_all(fetch)
 
     def loop(step, carry):
@@ -366,9 +378,18 @@
     return pl.pallas_call(
         functools.partial(prepare_kernel, slabs),
         in_specs=[HBM],
-        out_specs=[HBM, VMEM],
-        out_shape=[pltpu.HBM((128, 64, 128), F32), kept(128, 8, 128)],
-        scratch_shapes=[pltpu.VMEM((1024, 128), F32), pltpu.VMEM((128, 128), F32), BLOCKS_Q, BLOCKS_V, SEMS, SEMS],
+        out_specs=[HBM, HBM],
+        out_shape=[pltpu.HBM((128, 64, 128), F32), pltpu.HBM((128, 8, 128), F32)],
+        scratch_shapes=[
+            pltpu.VMEM((1024, 128), F32),
+            pltpu.VMEM((128, 128), F32),
+            BLOCKS_Q,
+            BLOCKS_V,
+            pltpu.VMEM((128, 8, 128), F32),
+            SEMS,
+            SEMS,
+            SEMS,
+        ],
         compiler_params=PARAMS,
         name="prepare",
     )(away(prior))

time: 78.4 us -> 78.2 us (level)
  Pallas kernels: 29.7 us -> 28.8 us
  transfers between devices with their start and end apart: 5 -> 5, of which waited for: 1 -> 1; matrix products, arithmetic and copies ran while one was open for 0% -> 0% of each run, Pallas kernels for 18% -> 17%
where the time goes in v6:
time: 78.2 us; the launch traced here: 77.2 us
  starting transfers between devices  34.3 us (44%)
  Pallas kernels  28.8 us (37%)
  blocking collectives  10.8 us (14%)
  waiting for transfers between devices  3.18 us (4%)
    all_to_all x2, starting transfers between devices, sum_over_velocities(): lax.all_to_all(partial_sums, 'vel', 0, 0, axis_index_groups=[ORDER])  19.8 us
    all_to_all x1, blocking collectives, sum_over_velocities(): lax.all_to_all(mixed, 'vel', 0, 0, axis_index_groups=[ORDER])  10.8 us
    all_to_all x1, starting transfers between devices, sum_over_velocities(): lax.all_to_all(mixed, 'vel', 0, 0, axis_index_groups=[ORDER])  9.55 us
    pallas_call x1, Pallas kernels, middle(): pl.pallas_call(functools.partial(middle_kernel, slabs), in_specs=[HBM, VM...  5.88 us
    pallas_call x1, Pallas kernels, prepare_next(): pl.pallas_call(functools.partial(prepare_next_kernel, slabs), in_specs=[H...  5.8 us
    pallas_call x1, Pallas kernels, last(): pl.pallas_call(functools.partial(last_kernel, slabs), in_specs=[HBM, VMEM...  5.48 us
    ppermute x2, starting transfers between devices, body(): recv = lax.ppermute(send, axes, pairs)  4.91 us
    pallas_call x1, Pallas kernels, prepare(): pl.pallas_call(functools.partial(prepare_kernel, slabs), in_specs=[HBM],...  4.6 us
  transfers between devices with their start and end apart: 5, of which 1 were waited for; matrix products, arithmetic and copies ran while one was open for 0% of the time, Pallas kernels for 17%

profile of v6, /device:TPU:1, one launch (start us, length us, event | category | flops | bytes accessed | tf_op | source)
XLA Modules:
  0.0 77.2 jit_solution(11600195956544837702)
XLA Ops:
  0.0 0.0 copy-start
  0.0 3.2 %first_moments.1 = f32[64,8,128]{2,1,0:T(8,128)} custom-call(f32[64,128,128]{2,1,0:T(8,128)} %bitcast.9), custom_call_target="tpu_custom_call" | custom-call | tf_op jit(solution)/shard_map/first_moments/pallas_call | solution.py:209
  3.2 11.7 %all-to-all-start = ((f32[32,16,128]{2,1,0:T(8,128)}), f32[32,16,128]{2,1,0:T(8,128)S(1)}, u32[]{:S(2)}, u32[]{:S(2)}) async-start(f32[32,16,128]{2,1,0:T(8,128)} %bitcast.13), calls=%async_computation | async-start | bytes 524288 | tf_op jit(solution)/shard_map/all_to_all | solution.py:272
  14.9 4.6 %prepare.1 = (f32[128,64,128]{2,1,0:T(8,128)}, f32[128,8,128]{2,1,0:T(8,128)}) custom-call(f32[64,128,128]{2,1,0:T(8,128)} %bitcast.10), custom_call_target="tpu_custom_call" | custom-call | tf_op jit(solution)/shard_map/prepare/pallas_call | solution.py:378
  19.5 0.0 all-to-all-done.gathered
  19.5 0.0 copy-done
  19.5 1.1 %mix_moments.2 = f32[32,16,128]{2,1,0:T(8,128)} custom-call(f32[256,256]{1,0:T(8,128)S(1)} %copy-done, f32[32,16,128]{2,1,0:T(8,128)S(1)} %all-to-all-done.gathered), custom_call_target="tpu_custom_call" | custom-call | tf_op jit(solution)/shard_map/mix_moments/pallas_call | solution.py:261
  20.6 3.0 %collective-permute-start = (f32[128,8,128]{2,1,0:T(8,128)}, f32[128,8,128]{2,1,0:T(8,128)S(1)}, u32[]{:S(2)}, u32[]{:S(2)}) collective-permute-start(f32[128,8,128]{2,1,0:T(8,128)} %get-tuple-element.26), channel_id=1, source_target_pairs={{16,48},{17,49},{18,50},{19,51},{20,52},{21,53},{22,54},{23,55},{2... | collective-permute-start | bytes 1572872 | tf_op jit(solution)/shard_map/ppermute | solution.py:620
  23.6 9.6 %all-to-all-start.1 = ((f32[32,16,128]{2,1,0:T(8,128)}), f32[32,16,128]{2,1,0:T(8,128)S(1)}, u32[]{:S(2)}, u32[]{:S(2)}) async-start(f32[32,16,128]{2,1,0:T(8,128)} %mix_moments.2), calls=%async_computation.1 | async-start | bytes 524288 | tf_op jit(solution)/shard_map/all_to_all | solution.py:276
  33.2 2.4 %pack.1.packed = bf16[128,64,128]{2,1,0:T(8,128)(2,1)S(1)} custom-call(f32[64,64,128]{2,1,0:T(8,128)} %bitcast.12), custom_call_target="tpu_custom_call" | custom-call | tf_op jit(solution)/shard_map/pack/pallas_call | solution.py:242
  35.6 3.2 %all-to-all-done.1 = f32[32,16,128]{2,1,0:T(8,128)S(1)} async-done(((f32[32,16,128]{2,1,0:T(8,128)}), f32[32,16,128]{2,1,0:T(8,128)S(1)}, u32[]{:S(2)}, u32[]{:S(2)}) %all-to-all-start.1) | async-done | bytes 262176 | tf_op jit(solution)/shard_map/all_to_all | solution.py:276
  38.8 0.0 collective-permute-done.recv
  38.8 5.9 %middle.1 = (f32[128,64,128]{2,1,0:T(8,128)}, f32[512,128]{1,0:T(8,128)}, f32[128,8,128]{2,1,0:T(8,128)}) custom-call(f32[128,64,128]{2,1,0:T(8,128)} %get-tuple-element.25.right_away, bf16[128,64,128]{2,1,0:T(8,128)(2,1)S(1)} %pack.1.packed, f32[128,8,128]{2,1,0:T(8,128)S(1)} %collective-permute-done.recv, f32[512,128]{1,0:T(8,128)S(1)} %bitcast.7), custom_call_target="tpu_custom_call" | custom-call | tf_op jit(solution)/shard_map/middle/pallas_call | solution.py:536
  44.6 1.9 %collective-permute-start.1 = (f32[128,8,128]{2,1,0:T(8,128)}, f32[128,8,128]{2,1,0:T(8,128)S(1)}, u32[]{:S(2)}, u32[]{:S(2)}) collective-permute-start(f32[128,8,128]{2,1,0:T(8,128)} %get-tuple-element.33), channel_id=1, source_target_pairs={{16,48},{17,49},{18,50},{19,51},{20,52},{21,53},{22,54},{23,55},{2... | collective-permute-start | bytes 1572872 | tf_op jit(solution)/shard_map/ppermute | solution.py:623
  46.6 8.1 %all-to-all-start.2 = ((f32[32,16,128]{2,1,0:T(8,128)}), f32[32,16,128]{2,1,0:T(8,128)S(1)}, u32[]{:S(2)}, u32[]{:S(2)}) async-start(f32[32,16,128]{2,1,0:T(8,128)} %bitcast.14), calls=%async_computation.2 | async-start | bytes 524288 | tf_op jit(solution)/shard_map/all_to_all | solution.py:272
  54.7 5.8 %prepare_next.1.right_away = f32[128,64,128]{2,1,0:T(8,128)} custom-call(f32[128,64,128]{2,1,0:T(8,128)} %get-tuple-element.29.fresh, f32[64,128,128]{2,1,0:T(8,128)} %bitcast.11), custom_call_target="tpu_custom_call" | custom-call | tf_op jit(solution)/shard_map/prepare_next/pallas_call | solution.py:428
  60.5 0.0 all-to-all-done.2.gathered
  60.5 0.4 mix_moments.3
  60.9 10.8 %all_to_all.20 = f32[32,16,128]{2,1,0:T(8,128)S(1)} all-to-all(f32[32,16,128]{2,1,0:T(8,128)S(1)} %mix_moments.3), channel_id=1, replica_groups={{26,30,27,25,22,31,29,24,23,21,18,28,20,19,17,16,10,14,11,9,6,15,13,8,7..., dimensions={0} | all-to-all | bytes 524288 | tf_op jit(solution)/shard_map/all_to_all | solution.py:276
  71.7 0.0 collective-permute-done.1.recv
  71.7 5.5 %last.1 = f32[64,128,128]{2,1,0:T(8,128)} custom-call(f32[128,64,128]{2,1,0:T(8,128)} %prepare_next.1.right_away, bf16[128,64,128]{2,1,0:T(8,128)(2,1)S(1)} %pack.1.packed, f32[128,8,128]{2,1,0:T(8,128)S(1)} %collective-permute-done.1.recv, f32[512,128]{1,0:T(8,128)S(1)} %bitcast.8), custom_call_target="tpu_custom_call" | custom-call | tf_op jit(solution)/shard_map/last/pallas_call | solution.py:585
Async XLA Ops:
  0.0 19.5 %copy-start = (f32[256,256]{1,0:T(8,128)S(1)}, f32[256,256]{1,0:T(8,128)}, u32[]{:S(2)}) copy-start(f32[256,256]{1,0:T(8,128)} %constant.2.clone.mix) | copy-start | bytes 786436
  3.2 16.3 %all-to-all-start = ((f32[32,16,128]{2,1,0:T(8,128)}), f32[32,16,128]{2,1,0:T(8,128)S(1)}, u32[]{:S(2)}, u32[]{:S(2)}) async-start(f32[32,16,128]{2,1,0:T(8,128)} %bitcast.13), calls=%async_computation | async-start | bytes 524288 | tf_op jit(solution)/shard_map/all_to_all | solution.py:272
  20.6 18.1 %collective-permute-start = (f32[128,8,128]{2,1,0:T(8,128)}, f32[128,8,128]{2,1,0:T(8,128)S(1)}, u32[]{:S(2)}, u32[]{:S(2)}) collective-permute-start(f32[128,8,128]{2,1,0:T(8,128)} %get-tuple-element.26), channel_id=1, source_target_pairs={{16,48},{17,49},{18,50},{19,51},{20,52},{21,53},{22,54},{23,55},{2... | collective-permute-start | bytes 1572872 | tf_op jit(solution)/shard_map/ppermute | solution.py:620
  23.6 15.1 %all-to-all-start.1 = ((f32[32,16,128]{2,1,0:T(8,128)}), f32[32,16,128]{2,1,0:T(8,128)S(1)}, u32[]{:S(2)}, u32[]{:S(2)}) async-start(f32[32,16,128]{2,1,0:T(8,128)} %mix_moments.2), calls=%async_computation.1 | async-start | bytes 524288 | tf_op jit(solution)/shard_map/all_to_all | solution.py:276
  44.6 27.1 %collective-permute-start.1 = (f32[128,8,128]{2,1,0:T(8,128)}, f32[128,8,128]{2,1,0:T(8,128)S(1)}, u32[]{:S(2)}, u32[]{:S(2)}) collective-permute-start(f32[128,8,128]{2,1,0:T(8,128)} %get-tuple-element.33), channel_id=1, source_target_pairs={{16,48},{17,49},{18,50},{19,51},{20,52},{21,53},{22,54},{23,55},{2... | collective-permute-start | bytes 1572872 | tf_op jit(solution)/shard_map/ppermute | solution.py:623
  46.6 13.9 %all-to-all-start.2 = ((f32[32,16,128]{2,1,0:T(8,128)}), f32[32,16,128]{2,1,0:T(8,128)S(1)}, u32[]{:S(2)}, u32[]{:S(2)}) async-start(f32[32,16,128]{2,1,0:T(8,128)} %bitcast.14), calls=%async_computation.2 | async-start | bytes 524288 | tf_op jit(solution)/shard_map/all_to_all | solution.py:272

commit v7 on v6

--- a/solution.py
+++ b/solution.py
@@ -272,7 +272,6 @@
     gathered = lax.all_to_all(partial_sums, "vel", 0, 0, axis_index_groups=[ORDER])
     gathered, beside = lax.optimization_barrier((gathered, beside))
     mixed = mix_moments(mix, gathered)
-    mixed, beside = lax.optimization_barrier((mixed, beside))
     return lax.all_to_all(mixed, "vel", 0, 0, axis_index_groups=[ORDER]).reshape(512, 128), beside
 
 

time: 78.2 us -> 77.7 us (level)
  waiting for transfers between devices: 3.18 us -> 2.11 us
  starting transfers between devices: 34.3 us -> 35.1 us
    all_to_all x1, waiting for transfers between devices: 3.17 us -> 2.1 us  [sum_over_velocities(): lax.all_to_all(mixed, 'vel', 0, 0, axis_index_groups=[ORDER])]
    all_to_all x2, starting transfers between devices: 19.8 us -> 20.6 us  [sum_over_velocities(): lax.all_to_all(partial_sums, 'vel', 0, 0, axis_index_groups=[ORDER])]
  transfers between devices with their start and end apart: 5 -> 5, of which waited for: 1 -> 1; matrix products, arithmetic and copies ran while one was open for 0% -> 0% of each run, Pallas kernels for 17% -> 18%
where the time goes in v7:
time: 77.7 us; the launch traced here: 77.2 us
  starting transfers between devices  35.1 us (45%)
  Pallas kernels  28.8 us (37%)
  blocking collectives  11.1 us (14%)
  waiting for transfers between devices  2.11 us (3%)
    all_to_all x2, starting transfers between devices, sum_over_velocities(): lax.all_to_all(partial_sums, 'vel', 0, 0, axis_index_groups=[ORDER])  20.6 us
    all_to_all x1, blocking collectives, sum_over_velocities(): lax.all_to_all(mixed, 'vel', 0, 0, axis_index_groups=[ORDER])  11.1 us
    all_to_all x1, starting transfers between devices, sum_over_velocities(): lax.all_to_all(mixed, 'vel', 0, 0, axis_index_groups=[ORDER])  9.54 us
    pallas_call x1, Pallas kernels, middle(): pl.pallas_call(functools.partial(middle_kernel, slabs), in_specs=[HBM, VM...  5.88 us
    pallas_call x1, Pallas kernels, prepare_next(): pl.pallas_call(functools.partial(prepare_next_kernel, slabs), in_specs=[H...  5.8 us
    pallas_call x1, Pallas kernels, last(): pl.pallas_call(functools.partial(last_kernel, slabs), in_specs=[HBM, VMEM...  5.48 us
    ppermute x2, starting transfers between devices, body(): recv = lax.ppermute(send, axes, pairs)  4.92 us
    pallas_call x1, Pallas kernels, prepare(): pl.pallas_call(functools.partial(prepare_kernel, slabs), in_specs=[HBM],...  4.6 us
  transfers between devices with their start and end apart: 5, of which 1 were waited for; matrix products, arithmetic and copies ran while one was open for 0% of the time, Pallas kernels for 18%

profile of v7, /device:TPU:1, one launch (start us, length us, event | category | flops | bytes accessed | tf_op | source)
XLA Modules:
  0.0 77.2 jit_solution(17933458761023715294)
XLA Ops:
  0.0 0.0 copy-start
  0.0 3.2 %first_moments.1 = f32[64,8,128]{2,1,0:T(8,128)} custom-call(f32[64,128,128]{2,1,0:T(8,128)} %bitcast.9), custom_call_target="tpu_custom_call" | custom-call | tf_op jit(solution)/shard_map/first_moments/pallas_call | solution.py:209
  3.2 11.7 %all-to-all-start = ((f32[32,16,128]{2,1,0:T(8,128)}), f32[32,16,128]{2,1,0:T(8,128)S(1)}, u32[]{:S(2)}, u32[]{:S(2)}) async-start(f32[32,16,128]{2,1,0:T(8,128)} %bitcast.13), calls=%async_computation | async-start | bytes 524288 | tf_op jit(solution)/shard_map/all_to_all | solution.py:272
  14.9 4.6 %prepare.1 = (f32[128,64,128]{2,1,0:T(8,128)}, f32[128,8,128]{2,1,0:T(8,128)}) custom-call(f32[64,128,128]{2,1,0:T(8,128)} %bitcast.10), custom_call_target="tpu_custom_call" | custom-call | tf_op jit(solution)/shard_map/prepare/pallas_call | solution.py:377
  19.5 0.0 all-to-all-done.gathered
  19.5 3.0 %collective-permute-start = (f32[128,8,128]{2,1,0:T(8,128)}, f32[128,8,128]{2,1,0:T(8,128)S(1)}, u32[]{:S(2)}, u32[]{:S(2)}) collective-permute-start(f32[128,8,128]{2,1,0:T(8,128)} %get-tuple-element.18), channel_id=1, source_target_pairs={{16,48},{17,49},{18,50},{19,51},{20,52},{21,53},{22,54},{23,55},{2... | collective-permute-start | bytes 1572872 | tf_op jit(solution)/shard_map/ppermute | solution.py:619
  22.5 0.0 copy-done
  22.5 1.1 %mix_moments.2 = f32[32,16,128]{2,1,0:T(8,128)} custom-call(f32[256,256]{1,0:T(8,128)S(1)} %copy-done, f32[32,16,128]{2,1,0:T(8,128)S(1)} %all-to-all-done.gathered), custom_call_target="tpu_custom_call" | custom-call | tf_op jit(solution)/shard_map/mix_moments/pallas_call | solution.py:261
  23.6 9.5 %all-to-all-start.1 = ((f32[32,16,128]{2,1,0:T(8,128)}), f32[32,16,128]{2,1,0:T(8,128)S(1)}, u32[]{:S(2)}, u32[]{:S(2)}) async-start(f32[32,16,128]{2,1,0:T(8,128)} %mix_moments.2), calls=%async_computation.1 | async-start | bytes 524288 | tf_op jit(solution)/shard_map/all_to_all | solution.py:275
  33.2 2.4 %pack.1.packed = bf16[128,64,128]{2,1,0:T(8,128)(2,1)S(1)} custom-call(f32[64,64,128]{2,1,0:T(8,128)} %bitcast.12), custom_call_target="tpu_custom_call" | custom-call | tf_op jit(solution)/shard_map/pack/pallas_call | solution.py:242
  35.6 2.1 %all-to-all-done.1 = f32[32,16,128]{2,1,0:T(8,128)S(1)} async-done(((f32[32,16,128]{2,1,0:T(8,128)}), f32[32,16,128]{2,1,0:T(8,128)S(1)}, u32[]{:S(2)}, u32[]{:S(2)}) %all-to-all-start.1) | async-done | bytes 262176 | tf_op jit(solution)/shard_map/all_to_all | solution.py:275
  37.7 0.0 collective-permute-done.recv
  37.7 5.9 %middle.1 = (f32[128,64,128]{2,1,0:T(8,128)}, f32[512,128]{1,0:T(8,128)}, f32[128,8,128]{2,1,0:T(8,128)}) custom-call(f32[128,64,128]{2,1,0:T(8,128)} %get-tuple-element.17.right_away, bf16[128,64,128]{2,1,0:T(8,128)(2,1)S(1)} %pack.1.packed, f32[128,8,128]{2,1,0:T(8,128)S(1)} %collective-permute-done.recv, f32[512,128]{1,0:T(8,128)S(1)} %bitcast.7), custom_call_target="tpu_custom_call" | custom-call | tf_op jit(solution)/shard_map/middle/pallas_call | solution.py:535
  43.6 1.9 %collective-permute-start.1 = (f32[128,8,128]{2,1,0:T(8,128)}, f32[128,8,128]{2,1,0:T(8,128)S(1)}, u32[]{:S(2)}, u32[]{:S(2)}) collective-permute-start(f32[128,8,128]{2,1,0:T(8,128)} %get-tuple-element.23), channel_id=1, source_target_pairs={{16,48},{17,49},{18,50},{19,51},{20,52},{21,53},{22,54},{23,55},{2... | collective-permute-start | bytes 1572872 | tf_op jit(solution)/shard_map/ppermute | solution.py:622
  45.5 8.9 %all-to-all-start.2 = ((f32[32,16,128]{2,1,0:T(8,128)}), f32[32,16,128]{2,1,0:T(8,128)S(1)}, u32[]{:S(2)}, u32[]{:S(2)}) async-start(f32[32,16,128]{2,1,0:T(8,128)} %bitcast.14), calls=%async_computation.2 | async-start | bytes 524288 | tf_op jit(solution)/shard_map/all_to_all | solution.py:272
  54.4 5.8 %prepare_next.1.right_away = f32[128,64,128]{2,1,0:T(8,128)} custom-call(f32[128,64,128]{2,1,0:T(8,128)} %get-tuple-element.21.fresh, f32[64,128,128]{2,1,0:T(8,128)} %bitcast.11), custom_call_target="tpu_custom_call" | custom-call | tf_op jit(solution)/shard_map/prepare_next/pallas_call | solution.py:427
  60.2 0.0 all-to-all-done.2.gathered
  60.2 0.4 mix_moments.3
  60.6 11.1 %all_to_all.20 = f32[32,16,128]{2,1,0:T(8,128)S(1)} all-to-all(f32[32,16,128]{2,1,0:T(8,128)S(1)} %mix_moments.3), channel_id=1, replica_groups={{26,30,27,25,22,31,29,24,23,21,18,28,20,19,17,16,10,14,11,9,6,15,13,8,7..., dimensions={0} | all-to-all | bytes 524288 | tf_op jit(solution)/shard_map/all_to_all | solution.py:275
  71.7 0.0 collective-permute-done.1.recv
  71.7 5.5 %last.1 = f32[64,128,128]{2,1,0:T(8,128)} custom-call(f32[128,64,128]{2,1,0:T(8,128)} %prepare_next.1.right_away, bf16[128,64,128]{2,1,0:T(8,128)(2,1)S(1)} %pack.1.packed, f32[128,8,128]{2,1,0:T(8,128)S(1)} %collective-permute-done.1.recv, f32[512,128]{1,0:T(8,128)S(1)} %bitcast.8), custom_call_target="tpu_custom_call" | custom-call | tf_op jit(solution)/shard_map/last/pallas_call | solution.py:584
Async XLA Ops:
  0.0 22.5 %copy-start = (f32[256,256]{1,0:T(8,128)S(1)}, f32[256,256]{1,0:T(8,128)}, u32[]{:S(2)}) copy-start(f32[256,256]{1,0:T(8,128)} %constant.2.clone.mix) | copy-start | bytes 786436
  3.2 16.3 %all-to-all-start = ((f32[32,16,128]{2,1,0:T(8,128)}), f32[32,16,128]{2,1,0:T(8,128)S(1)}, u32[]{:S(2)}, u32[]{:S(2)}) async-start(f32[32,16,128]{2,1,0:T(8,128)} %bitcast.13), calls=%async_computation | async-start | bytes 524288 | tf_op jit(solution)/shard_map/all_to_all | solution.py:272
  19.5 18.2 %collective-permute-start = (f32[128,8,128]{2,1,0:T(8,128)}, f32[128,8,128]{2,1,0:T(8,128)S(1)}, u32[]{:S(2)}, u32[]{:S(2)}) collective-permute-start(f32[128,8,128]{2,1,0:T(8,128)} %get-tuple-element.18), channel_id=1, source_target_pairs={{16,48},{17,49},{18,50},{19,51},{20,52},{21,53},{22,54},{23,55},{2... | collective-permute-start | bytes 1572872 | tf_op jit(solution)/shard_map/ppermute | solution.py:619
  23.6 14.1 %all-to-all-start.1 = ((f32[32,16,128]{2,1,0:T(8,128)}), f32[32,16,128]{2,1,0:T(8,128)S(1)}, u32[]{:S(2)}, u32[]{:S(2)}) async-start(f32[32,16,128]{2,1,0:T(8,128)} %mix_moments.2), calls=%async_computation.1 | async-start | bytes 524288 | tf_op jit(solution)/shard_map/all_to_all | solution.py:275
  43.6 28.2 %collective-permute-start.1 = (f32[128,8,128]{2,1,0:T(8,128)}, f32[128,8,128]{2,1,0:T(8,128)S(1)}, u32[]{:S(2)}, u32[]{:S(2)}) collective-permute-start(f32[128,8,128]{2,1,0:T(8,128)} %get-tuple-element.23), channel_id=1, source_target_pairs={{16,48},{17,49},{18,50},{19,51},{20,52},{21,53},{22,54},{23,55},{2... | collective-permute-start | bytes 1572872 | tf_op jit(solution)/shard_map/ppermute | solution.py:622
  45.5 14.7 %all-to-all-start.2 = ((f32[32,16,128]{2,1,0:T(8,128)}), f32[32,16,128]{2,1,0:T(8,128)S(1)}, u32[]{:S(2)}, u32[]{:S(2)}) async-start(f32[32,16,128]{2,1,0:T(8,128)} %bitcast.14), calls=%async_computation.2 | async-start | bytes 524288 | tf_op jit(solution)/shard_map/all_to_all | solution.py:272

commit v8 on v7

--- a/solution.py
+++ b/solution.py
@@ -16,7 +16,6 @@
 VEL = 32
 LOCAL_Y = 8
 HIGH = [float(np.sqrt(k + 0.5)) for k in range(4)]
-HIGHEST = lax.Precision.HIGHEST
 F32 = jnp.float32
 BF16 = jnp.bfloat16
 HALF = 64
@@ -252,7 +251,8 @@
 
 def mix_kernel(mix, gathered, mixed):
     part = jnp.concatenate([gathered[:, low * 8 : low * 8 + 8, :].reshape(VEL * 8, 128) for low in range(2)], axis=1)
-    result = jnp.dot(mix[...], part, preferred_element_type=F32, precision=HIGHEST)
+    hi, lo = split(part)
+    result = jnp.dot(mix[...], jnp.concatenate([hi, hi, lo], axis=0), preferred_element_type=F32)
     for low in range(2):
         mixed[:, low * 8 : low * 8 + 8, :] = result[:, low * 128 : low * 128 + 128].reshape(VEL, 8, 128)
 
@@ -610,7 +610,9 @@
 
 
 def body(slabs, prior, block_inverse):
-    mix = jnp.asarray(MIX)
+    leading = MIX.astype(jnp.bfloat16)
+    rest = (MIX - leading.astype(np.float32)).astype(jnp.bfloat16)
+    mix = jnp.asarray(np.concatenate([leading, rest, leading], axis=1))
     axes = ("sp", "vel")
     pairs = halo_pairs(slabs)
     cells = prior.reshape(64, 128, 128)

time: 77.7 us -> 77.4 us (level)
  no operation moved by 1% of the time
where the time goes in v8:
time: 77.4 us; the launch traced here: 77 us
  starting transfers between devices  35 us (45%)
  Pallas kernels  28.6 us (37%)
  blocking collectives  11.1 us (14%)
  waiting for transfers between devices  2.22 us (3%)
    all_to_all x2, starting transfers between devices, sum_over_velocities(): lax.all_to_all(partial_sums, 'vel', 0, 0, axis_index_groups=[ORDER])  20.5 us
    all_to_all x1, blocking collectives, sum_over_velocities(): lax.all_to_all(mixed, 'vel', 0, 0, axis_index_groups=[ORDER])  11.1 us
    all_to_all x1, starting transfers between devices, sum_over_velocities(): lax.all_to_all(mixed, 'vel', 0, 0, axis_index_groups=[ORDER])  9.54 us
    pallas_call x1, Pallas kernels, middle(): pl.pallas_call(functools.partial(middle_kernel, slabs), in_specs=[HBM, VM...  5.88 us
    pallas_call x1, Pallas kernels, prepare_next(): pl.pallas_call(functools.partial(prepare_next_kernel, slabs), in_specs=[H...  5.8 us
    pallas_call x1, Pallas kernels, last(): pl.pallas_call(functools.partial(last_kernel, slabs), in_specs=[HBM, VMEM...  5.48 us
    ppermute x2, starting transfers between devices, body(): recv = lax.ppermute(send, axes, pairs)  4.92 us
    pallas_call x1, Pallas kernels, prepare(): pl.pallas_call(functools.partial(prepare_kernel, slabs), in_specs=[HBM],...  4.6 us
  transfers between devices with their start and end apart: 5, of which 1 were waited for; matrix products, arithmetic and copies ran while one was open for 0% of the time, Pallas kernels for 18%

profile of v8, /device:TPU:1, one launch (start us, length us, event | category | flops | bytes accessed | tf_op | source)
XLA Modules:
  0.0 77.0 jit_solution(5491912721036493179)
XLA Ops:
  0.0 0.0 copy-start
  0.0 3.2 %first_moments.1 = f32[64,8,128]{2,1,0:T(8,128)} custom-call(f32[64,128,128]{2,1,0:T(8,128)} %bitcast.9), custom_call_target="tpu_custom_call" | custom-call | tf_op jit(solution)/shard_map/first_moments/pallas_call | solution.py:208
  3.2 11.7 %all-to-all-start = ((f32[32,16,128]{2,1,0:T(8,128)}), f32[32,16,128]{2,1,0:T(8,128)S(1)}, u32[]{:S(2)}, u32[]{:S(2)}) async-start(f32[32,16,128]{2,1,0:T(8,128)} %bitcast.13), calls=%async_computation | async-start | bytes 524288 | tf_op jit(solution)/shard_map/all_to_all | solution.py:272
  14.9 4.6 %prepare.1 = (f32[128,64,128]{2,1,0:T(8,128)}, f32[128,8,128]{2,1,0:T(8,128)}) custom-call(f32[64,128,128]{2,1,0:T(8,128)} %bitcast.10), custom_call_target="tpu_custom_call" | custom-call | tf_op jit(solution)/shard_map/prepare/pallas_call | solution.py:377
  19.5 0.0 all-to-all-done.gathered
  19.5 3.0 %collective-permute-start = (f32[128,8,128]{2,1,0:T(8,128)}, f32[128,8,128]{2,1,0:T(8,128)S(1)}, u32[]{:S(2)}, u32[]{:S(2)}) collective-permute-start(f32[128,8,128]{2,1,0:T(8,128)} %get-tuple-element.18), channel_id=1, source_target_pairs={{16,48},{17,49},{18,50},{19,51},{20,52},{21,53},{22,54},{23,55},{2... | collective-permute-start | bytes 1572872 | tf_op jit(solution)/shard_map/ppermute | solution.py:621
  22.5 0.0 copy-done
  22.5 1.0 %mix_moments.2 = f32[32,16,128]{2,1,0:T(8,128)} custom-call(bf16[256,768]{1,0:T(8,128)(2,1)S(1)} %copy-done, f32[32,16,128]{2,1,0:T(8,128)S(1)} %all-to-all-done.gathered), custom_call_target="tpu_custom_call" | custom-call | tf_op jit(solution)/shard_map/mix_moments/pallas_call | solution.py:261
  23.5 9.5 %all-to-all-start.1 = ((f32[32,16,128]{2,1,0:T(8,128)}), f32[32,16,128]{2,1,0:T(8,128)S(1)}, u32[]{:S(2)}, u32[]{:S(2)}) async-start(f32[32,16,128]{2,1,0:T(8,128)} %mix_moments.2), calls=%async_computation.1 | async-start | bytes 524288 | tf_op jit(solution)/shard_map/all_to_all | solution.py:275
  33.1 2.4 %pack.1.packed = bf16[128,64,128]{2,1,0:T(8,128)(2,1)S(1)} custom-call(f32[64,64,128]{2,1,0:T(8,128)} %bitcast.12), custom_call_target="tpu_custom_call" | custom-call | tf_op jit(solution)/shard_map/pack/pallas_call | solution.py:241
  35.5 2.2 %all-to-all-done.1 = f32[32,16,128]{2,1,0:T(8,128)S(1)} async-done(((f32[32,16,128]{2,1,0:T(8,128)}), f32[32,16,128]{2,1,0:T(8,128)S(1)}, u32[]{:S(2)}, u32[]{:S(2)}) %all-to-all-start.1) | async-done | bytes 262176 | tf_op jit(solution)/shard_map/all_to_all | solution.py:275
  37.7 0.0 collective-permute-done.recv
  37.7 5.9 %middle.1 = (f32[128,64,128]{2,1,0:T(8,128)}, f32[512,128]{1,0:T(8,128)}, f32[128,8,128]{2,1,0:T(8,128)}) custom-call(f32[128,64,128]{2,1,0:T(8,128)} %get-tuple-element.17.right_away, bf16[128,64,128]{2,1,0:T(8,128)(2,1)S(1)} %pack.1.packed, f32[128,8,128]{2,1,0:T(8,128)S(1)} %collective-permute-done.recv, f32[512,128]{1,0:T(8,128)S(1)} %bitcast.7), custom_call_target="tpu_custom_call" | custom-call | tf_op jit(solution)/shard_map/middle/pallas_call | solution.py:535
  43.6 1.9 %collective-permute-start.1 = (f32[128,8,128]{2,1,0:T(8,128)}, f32[128,8,128]{2,1,0:T(8,128)S(1)}, u32[]{:S(2)}, u32[]{:S(2)}) collective-permute-start(f32[128,8,128]{2,1,0:T(8,128)} %get-tuple-element.23), channel_id=1, source_target_pairs={{16,48},{17,49},{18,50},{19,51},{20,52},{21,53},{22,54},{23,55},{2... | collective-permute-start | bytes 1572872 | tf_op jit(solution)/shard_map/ppermute | solution.py:624
  45.5 8.8 %all-to-all-start.2 = ((f32[32,16,128]{2,1,0:T(8,128)}), f32[32,16,128]{2,1,0:T(8,128)S(1)}, u32[]{:S(2)}, u32[]{:S(2)}) async-start(f32[32,16,128]{2,1,0:T(8,128)} %bitcast.14), calls=%async_computation.2 | async-start | bytes 524288 | tf_op jit(solution)/shard_map/all_to_all | solution.py:272
  54.3 5.8 %prepare_next.1.right_away = f32[128,64,128]{2,1,0:T(8,128)} custom-call(f32[128,64,128]{2,1,0:T(8,128)} %get-tuple-element.21.fresh, f32[64,128,128]{2,1,0:T(8,128)} %bitcast.11), custom_call_target="tpu_custom_call" | custom-call | tf_op jit(solution)/shard_map/prepare_next/pallas_call | solution.py:427
  60.1 0.0 all-to-all-done.2.gathered
  60.1 0.3 mix_moments.3
  60.4 11.1 %all_to_all.20 = f32[32,16,128]{2,1,0:T(8,128)S(1)} all-to-all(f32[32,16,128]{2,1,0:T(8,128)S(1)} %mix_moments.3), channel_id=1, replica_groups={{26,30,27,25,22,31,29,24,23,21,18,28,20,19,17,16,10,14,11,9,6,15,13,8,7..., dimensions={0} | all-to-all | bytes 524288 | tf_op jit(solution)/shard_map/all_to_all | solution.py:275
  71.5 0.0 collective-permute-done.1.recv
  71.5 5.5 %last.1 = f32[64,128,128]{2,1,0:T(8,128)} custom-call(f32[128,64,128]{2,1,0:T(8,128)} %prepare_next.1.right_away, bf16[128,64,128]{2,1,0:T(8,128)(2,1)S(1)} %pack.1.packed, f32[128,8,128]{2,1,0:T(8,128)S(1)} %collective-permute-done.1.recv, f32[512,128]{1,0:T(8,128)S(1)} %bitcast.8), custom_call_target="tpu_custom_call" | custom-call | tf_op jit(solution)/shard_map/last/pallas_call | solution.py:584
Async XLA Ops:
  0.0 22.5 %copy-start = (bf16[256,768]{1,0:T(8,128)(2,1)S(1)}, bf16[256,768]{1,0:T(8,128)(2,1)}, u32[]{:S(2)}) copy-start(bf16[256,768]{1,0:T(8,128)(2,1)} %constant.2.clone.mix) | copy-start | bytes 1179652
  3.2 16.3 %all-to-all-start = ((f32[32,16,128]{2,1,0:T(8,128)}), f32[32,16,128]{2,1,0:T(8,128)S(1)}, u32[]{:S(2)}, u32[]{:S(2)}) async-start(f32[32,16,128]{2,1,0:T(8,128)} %bitcast.13), calls=%async_computation | async-start | bytes 524288 | tf_op jit(solution)/shard_map/all_to_all | solution.py:272
  19.5 18.2 %collective-permute-start = (f32[128,8,128]{2,1,0:T(8,128)}, f32[128,8,128]{2,1,0:T(8,128)S(1)}, u32[]{:S(2)}, u32[]{:S(2)}) collective-permute-start(f32[128,8,128]{2,1,0:T(8,128)} %get-tuple-element.18), channel_id=1, source_target_pairs={{16,48},{17,49},{18,50},{19,51},{20,52},{21,53},{22,54},{23,55},{2... | collective-permute-start | bytes 1572872 | tf_op jit(solution)/shard_map/ppermute | solution.py:621
  23.5 14.2 %all-to-all-start.1 = ((f32[32,16,128]{2,1,0:T(8,128)}), f32[32,16,128]{2,1,0:T(8,128)S(1)}, u32[]{:S(2)}, u32[]{:S(2)}) async-start(f32[32,16,128]{2,1,0:T(8,128)} %mix_moments.2), calls=%async_computation.1 | async-start | bytes 524288 | tf_op jit(solution)/shard_map/all_to_all | solution.py:275
  43.6 27.9 %collective-permute-start.1 = (f32[128,8,128]{2,1,0:T(8,128)}, f32[128,8,128]{2,1,0:T(8,128)S(1)}, u32[]{:S(2)}, u32[]{:S(2)}) collective-permute-start(f32[128,8,128]{2,1,0:T(8,128)} %get-tuple-element.23), channel_id=1, source_target_pairs={{16,48},{17,49},{18,50},{19,51},{20,52},{21,53},{22,54},{23,55},{2... | collective-permute-start | bytes 1572872 | tf_op jit(solution)/shard_map/ppermute | solution.py:624
  45.5 14.6 %all-to-all-start.2 = ((f32[32,16,128]{2,1,0:T(8,128)}), f32[32,16,128]{2,1,0:T(8,128)S(1)}, u32[]{:S(2)}, u32[]{:S(2)}) async-start(f32[32,16,128]{2,1,0:T(8,128)} %bitcast.14), calls=%async_computation.2 | async-start | bytes 524288 | tf_op jit(solution)/shard_map/all_to_all | solution.py:272

commit v9 on v8

--- a/solution.py
+++ b/solution.py
@@ -575,7 +575,8 @@
         put(step)
         return carry
 
-    lax.fori_loop(0, 8, loop, 0)
+    for step in range(8):
+        loop(step, 0)
     for step in range(8):
         finish(step)
 

time: 77.4 us -> 77.5 us (level)
  no operation moved by 1% of the time
where the time goes in v9:
time: 77.5 us; the launch traced here: 77 us
  starting transfers between devices  35 us (45%)
  Pallas kernels  28.6 us (37%)
  blocking collectives  11.1 us (14%)
  waiting for transfers between devices  2.22 us (3%)
    all_to_all x2, starting transfers between devices, sum_over_velocities(): lax.all_to_all(partial_sums, 'vel', 0, 0, axis_index_groups=[ORDER])  20.5 us
    all_to_all x1, blocking collectives, sum_over_velocities(): lax.all_to_all(mixed, 'vel', 0, 0, axis_index_groups=[ORDER])  11.1 us
    all_to_all x1, starting transfers between devices, sum_over_velocities(): lax.all_to_all(mixed, 'vel', 0, 0, axis_index_groups=[ORDER])  9.54 us
    pallas_call x1, Pallas kernels, middle(): pl.pallas_call(functools.partial(middle_kernel, slabs), in_specs=[HBM, VM...  5.88 us
    pallas_call x1, Pallas kernels, prepare_next(): pl.pallas_call(functools.partial(prepare_next_kernel, slabs), in_specs=[H...  5.8 us
    pallas_call x1, Pallas kernels, last(): pl.pallas_call(functools.partial(last_kernel, slabs), in_specs=[HBM, VMEM...  5.51 us
    ppermute x2, starting transfers between devices, body(): recv = lax.ppermute(send, axes, pairs)  4.92 us
    pallas_call x1, Pallas kernels, prepare(): pl.pallas_call(functools.partial(prepare_kernel, slabs), in_specs=[HBM],...  4.6 us
  transfers between devices with their start and end apart: 5, of which 1 were waited for; matrix products, arithmetic and copies ran while one was open for 0% of the time, Pallas kernels for 18%

profile of v9, /device:TPU:1, one launch (start us, length us, event | category | flops | bytes accessed | tf_op | source)
XLA Modules:
  0.0 77.0 jit_solution(7084748203043182336)
XLA Ops:
  0.0 0.0 copy-start
  0.0 3.2 %first_moments.1 = f32[64,8,128]{2,1,0:T(8,128)} custom-call(f32[64,128,128]{2,1,0:T(8,128)} %bitcast.9), custom_call_target="tpu_custom_call" | custom-call | tf_op jit(solution)/shard_map/first_moments/pallas_call | solution.py:208
  3.2 11.7 %all-to-all-start = ((f32[32,16,128]{2,1,0:T(8,128)}), f32[32,16,128]{2,1,0:T(8,128)S(1)}, u32[]{:S(2)}, u32[]{:S(2)}) async-start(f32[32,16,128]{2,1,0:T(8,128)} %bitcast.13), calls=%async_computation | async-start | bytes 524288 | tf_op jit(solution)/shard_map/all_to_all | solution.py:272
  14.9 4.6 %prepare.1 = (f32[128,64,128]{2,1,0:T(8,128)}, f32[128,8,128]{2,1,0:T(8,128)}) custom-call(f32[64,128,128]{2,1,0:T(8,128)} %bitcast.10), custom_call_target="tpu_custom_call" | custom-call | tf_op jit(solution)/shard_map/prepare/pallas_call | solution.py:377
  19.5 0.0 all-to-all-done.gathered
  19.5 3.0 %collective-permute-start = (f32[128,8,128]{2,1,0:T(8,128)}, f32[128,8,128]{2,1,0:T(8,128)S(1)}, u32[]{:S(2)}, u32[]{:S(2)}) collective-permute-start(f32[128,8,128]{2,1,0:T(8,128)} %get-tuple-element.18), channel_id=1, source_target_pairs={{16,48},{17,49},{18,50},{19,51},{20,52},{21,53},{22,54},{23,55},{2... | collective-permute-start | bytes 1572872 | tf_op jit(solution)/shard_map/ppermute | solution.py:622
  22.5 0.0 copy-done
  22.5 1.0 %mix_moments.2 = f32[32,16,128]{2,1,0:T(8,128)} custom-call(bf16[256,768]{1,0:T(8,128)(2,1)S(1)} %copy-done, f32[32,16,128]{2,1,0:T(8,128)S(1)} %all-to-all-done.gathered), custom_call_target="tpu_custom_call" | custom-call | tf_op jit(solution)/shard_map/mix_moments/pallas_call | solution.py:261
  23.5 9.5 %all-to-all-start.1 = ((f32[32,16,128]{2,1,0:T(8,128)}), f32[32,16,128]{2,1,0:T(8,128)S(1)}, u32[]{:S(2)}, u32[]{:S(2)}) async-start(f32[32,16,128]{2,1,0:T(8,128)} %mix_moments.2), calls=%async_computation.1 | async-start | bytes 524288 | tf_op jit(solution)/shard_map/all_to_all | solution.py:275
  33.1 2.4 %pack.1.packed = bf16[128,64,128]{2,1,0:T(8,128)(2,1)S(1)} custom-call(f32[64,64,128]{2,1,0:T(8,128)} %bitcast.12), custom_call_target="tpu_custom_call" | custom-call | tf_op jit(solution)/shard_map/pack/pallas_call | solution.py:241
  35.5 2.2 %all-to-all-done.1 = f32[32,16,128]{2,1,0:T(8,128)S(1)} async-done(((f32[32,16,128]{2,1,0:T(8,128)}), f32[32,16,128]{2,1,0:T(8,128)S(1)}, u32[]{:S(2)}, u32[]{:S(2)}) %all-to-all-start.1) | async-done | bytes 262176 | tf_op jit(solution)/shard_map/all_to_all | solution.py:275
  37.7 0.0 collective-permute-done.recv
  37.7 5.9 %middle.1 = (f32[128,64,128]{2,1,0:T(8,128)}, f32[512,128]{1,0:T(8,128)}, f32[128,8,128]{2,1,0:T(8,128)}) custom-call(f32[128,64,128]{2,1,0:T(8,128)} %get-tuple-element.17.right_away, bf16[128,64,128]{2,1,0:T(8,128)(2,1)S(1)} %pack.1.packed, f32[128,8,128]{2,1,0:T(8,128)S(1)} %collective-permute-done.recv, f32[512,128]{1,0:T(8,128)S(1)} %bitcast.7), custom_call_target="tpu_custom_call" | custom-call | tf_op jit(solution)/shard_map/middle/pallas_call | solution.py:535
  43.6 1.9 %collective-permute-start.1 = (f32[128,8,128]{2,1,0:T(8,128)}, f32[128,8,128]{2,1,0:T(8,128)S(1)}, u32[]{:S(2)}, u32[]{:S(2)}) collective-permute-start(f32[128,8,128]{2,1,0:T(8,128)} %get-tuple-element.23), channel_id=1, source_target_pairs={{16,48},{17,49},{18,50},{19,51},{20,52},{21,53},{22,54},{23,55},{2... | collective-permute-start | bytes 1572872 | tf_op jit(solution)/shard_map/ppermute | solution.py:625
  45.5 8.8 %all-to-all-start.2 = ((f32[32,16,128]{2,1,0:T(8,128)}), f32[32,16,128]{2,1,0:T(8,128)S(1)}, u32[]{:S(2)}, u32[]{:S(2)}) async-start(f32[32,16,128]{2,1,0:T(8,128)} %bitcast.14), calls=%async_computation.2 | async-start | bytes 524288 | tf_op jit(solution)/shard_map/all_to_all | solution.py:272
  54.3 5.8 %prepare_next.1.right_away = f32[128,64,128]{2,1,0:T(8,128)} custom-call(f32[128,64,128]{2,1,0:T(8,128)} %get-tuple-element.21.fresh, f32[64,128,128]{2,1,0:T(8,128)} %bitcast.11), custom_call_target="tpu_custom_call" | custom-call | tf_op jit(solution)/shard_map/prepare_next/pallas_call | solution.py:427
  60.1 0.0 all-to-all-done.2.gathered
  60.1 0.3 mix_moments.3
  60.4 11.1 %all_to_all.20 = f32[32,16,128]{2,1,0:T(8,128)S(1)} all-to-all(f32[32,16,128]{2,1,0:T(8,128)S(1)} %mix_moments.3), channel_id=1, replica_groups={{26,30,27,25,22,31,29,24,23,21,18,28,20,19,17,16,10,14,11,9,6,15,13,8,7..., dimensions={0} | all-to-all | bytes 524288 | tf_op jit(solution)/shard_map/all_to_all | solution.py:275
  71.5 0.0 collective-permute-done.1.recv
  71.5 5.5 %last.1 = f32[64,128,128]{2,1,0:T(8,128)} custom-call(f32[128,64,128]{2,1,0:T(8,128)} %prepare_next.1.right_away, bf16[128,64,128]{2,1,0:T(8,128)(2,1)S(1)} %pack.1.packed, f32[128,8,128]{2,1,0:T(8,128)S(1)} %collective-permute-done.1.recv, f32[512,128]{1,0:T(8,128)S(1)} %bitcast.8), custom_call_target="tpu_custom_call" | custom-call | tf_op jit(solution)/shard_map/last/pallas_call | solution.py:585
Async XLA Ops:
  0.0 22.5 %copy-start = (bf16[256,768]{1,0:T(8,128)(2,1)S(1)}, bf16[256,768]{1,0:T(8,128)(2,1)}, u32[]{:S(2)}) copy-start(bf16[256,768]{1,0:T(8,128)(2,1)} %constant.2.clone.mix) | copy-start | bytes 1179652
  3.2 16.3 %all-to-all-start = ((f32[32,16,128]{2,1,0:T(8,128)}), f32[32,16,128]{2,1,0:T(8,128)S(1)}, u32[]{:S(2)}, u32[]{:S(2)}) async-start(f32[32,16,128]{2,1,0:T(8,128)} %bitcast.13), calls=%async_computation | async-start | bytes 524288 | tf_op jit(solution)/shard_map/all_to_all | solution.py:272
  19.5 18.2 %collective-permute-start = (f32[128,8,128]{2,1,0:T(8,128)}, f32[128,8,128]{2,1,0:T(8,128)S(1)}, u32[]{:S(2)}, u32[]{:S(2)}) collective-permute-start(f32[128,8,128]{2,1,0:T(8,128)} %get-tuple-element.18), channel_id=1, source_target_pairs={{16,48},{17,49},{18,50},{19,51},{20,52},{21,53},{22,54},{23,55},{2... | collective-permute-start | bytes 1572872 | tf_op jit(solution)/shard_map/ppermute | solution.py:622
  23.5 14.2 %all-to-all-start.1 = ((f32[32,16,128]{2,1,0:T(8,128)}), f32[32,16,128]{2,1,0:T(8,128)S(1)}, u32[]{:S(2)}, u32[]{:S(2)}) async-start(f32[32,16,128]{2,1,0:T(8,128)} %mix_moments.2), calls=%async_computation.1 | async-start | bytes 524288 | tf_op jit(solution)/shard_map/all_to_all | solution.py:275
  43.6 27.9 %collective-permute-start.1 = (f32[128,8,128]{2,1,0:T(8,128)}, f32[128,8,128]{2,1,0:T(8,128)S(1)}, u32[]{:S(2)}, u32[]{:S(2)}) collective-permute-start(f32[128,8,128]{2,1,0:T(8,128)} %get-tuple-element.23), channel_id=1, source_target_pairs={{16,48},{17,49},{18,50},{19,51},{20,52},{21,53},{22,54},{23,55},{2... | collective-permute-start | bytes 1572872 | tf_op jit(solution)/shard_map/ppermute | solution.py:625
  45.5 14.6 %all-to-all-start.2 = ((f32[32,16,128]{2,1,0:T(8,128)}), f32[32,16,128]{2,1,0:T(8,128)S(1)}, u32[]{:S(2)}, u32[]{:S(2)}) async-start(f32[32,16,128]{2,1,0:T(8,128)} %bitcast.14), calls=%async_computation.2 | async-start | bytes 524288 | tf_op jit(solution)/shard_map/all_to_all | solution.py:272
